TPU v7x, 256 devices: a whole 4x4x8 slice. The times are simulated.
256 devices in a mesh: seq: 16 (over x, y), tp: 8 (over z), rep: 2 (over core).
Axes of the slice: x: 4, y: 4, z: 8, core: 2. Of those that a mesh axis runs over, the one named last changes fastest.
Arguments:
- light_query: bfloat16 [32768, 8192], P(('seq', 'rep'), 'tp'), may hold values from -6 to 6
- light_key: bfloat16 [32768, 8192], P(('seq', 'rep'), 'tp'), may hold values from -6 to 6
- light_value: bfloat16 [32768, 8192], P(('seq', 'rep'), 'tp'), may hold values from -6 to 6
- log_decay: float32 [32768, 64], P(('seq', 'rep'), 'tp'), may hold values from -0.8 to 0
- prompt_pages: int32 [4], replicated, may hold values from 1 to 64, 128 in all
- norm_gain: float32 [8192], P('tp'), may hold values from 0.5 to 1.5
- cache_keys: bfloat16 [32768, 1024], P(('seq', 'rep'), 'tp'), may hold values from -6 to 6
- cache_values: bfloat16 [32768, 1024], P(('seq', 'rep'), 'tp'), may hold values from -6 to 6
- step_query: bfloat16 [2, 4, 4, 8192], P('rep', None, None, 'tp'), may hold values from -6 to 6
- step_key: bfloat16 [2, 4, 4, 8192], P('rep', None, None, 'tp'), may hold values from -6 to 6
- step_value: bfloat16 [2, 4, 4, 8192], P('rep', None, None, 'tp'), may hold values from -6 to 6
- step_decay: float32 [2, 4, 4, 64], P('rep', None, None, 'tp'), may hold values from -3 to -0.2
- soft_query: bfloat16 [2, 4, 4, 8192], P('rep', None, None, 'tp'), may hold values from -256 to 256
- soft_key: bfloat16 [2, 4, 4, 1024], P('rep', None, None, 'tp'), may hold values from -15 to 15
- soft_value: bfloat16 [2, 4, 4, 1024], P('rep', None, None, 'tp'), may hold values from -6 to 6
Outputs:
- light_out: bfloat16 [32768, 8192], P(('seq', 'rep'), 'tp')
- light_decode: bfloat16 [2, 4, 4, 64, 128], P('rep', None, None, 'tp', 'seq')
- soft_decode: bfloat16 [2, 4, 4, 8192], P('rep', None, None, 'tp')
Inputs may be any that keep to these rules, and one draw needn't show every extreme that they name: `prompt_pages`: the prompts are laid end to end in order and fill all 128 pages; the longest has exactly 64 pages.
All inputs are finite; a program needn't handle non-finite values.
Results may differ from a plain program's by a relative error of at most 0.014.
Values may be sent and summed in bfloat16 or wider, within the bound.
A program may use at most 128 MiB of HBM per device.

v0:
```python
import jax
import jax.numpy as jnp
from jax import lax
from jax.sharding import PartitionSpec as P

DH = 128
PAGE = 256
BLK = 512


norm_eps = 1e-06
mask_low = -1e30
highest = lax.Precision.HIGHEST


def carried_in(value, axis, join, neutral):
    place = lax.axis_index(axis)
    gathered = jax.tree.map(
        lambda a, kind: lax.all_gather(a.astype(kind), axis), value, (jnp.bfloat16, jnp.bfloat16)
    )
    state = jax.tree.map(lambda a, e: jnp.zeros_like(a) + jnp.asarray(e, a.dtype), value, neutral)

    def one(hop, state):
        return join(
            state,
            jax.tree.map(
                lambda a, own: lax.dynamic_index_in_dim(a, hop, 0, False).astype(own.dtype),
                gathered,
                value,
            ),
        )

    return lax.fori_loop(0, place, one, state)


def from_partner(value, axis, stride):
    return lax.ppermute(value, axis, [(i, i ^ 1 << stride) for i in range(lax.axis_size(axis))])


def combined_all(part, axis, combine):
    gathered = jax.tree.map(lambda a: lax.all_gather(a, axis), part)

    def take(source):
        return jax.tree.map(lambda a: lax.dynamic_index_in_dim(a, source, 0, False), gathered)

    return lax.fori_loop(
        1, lax.axis_size(axis), lambda source, state: combine(state, take(source)), take(0)
    )


def token_docs(prompt_pages, positions):
    page_ends = PAGE * jnp.cumsum(prompt_pages)
    return jnp.sum((positions[:, None] >= page_ends[None, :]).astype(jnp.int32), axis=1)


def join_summaries(earlier, later):
    return (earlier[0] * later[0], later[0][:, None, None] * earlier[1] + later[1])


def combine_partials(first_part, second_part):
    peak = jnp.maximum(first_part[0], second_part[0])
    first_scale = jnp.exp(first_part[0] - peak)
    second_scale = jnp.exp(second_part[0] - peak)
    return (
        peak,
        first_part[1] * first_scale + second_part[1] * second_scale,
        first_part[2] * first_scale[..., None] + second_part[2] * second_scale[..., None],
    )


def decode_steps(running, step_q, step_k, step_v, decay_rows):
    results = []
    for step_id in range(step_q.shape[1]):
        running = jnp.exp(decay_rows[:, step_id, :])[:, :, None, None] * running + jnp.einsum(
            "phd,phf->phdf", step_k[:, step_id], step_v[:, step_id]
        )
        results.append(jnp.einsum("phd,phdf->phf", step_q[:, step_id], running, precision=highest))
    return jnp.stack(results, axis=1)


def local_blocks(queries, key_rows, value_rows, decay_log, doc_ids, doc_before):
    row_count, head_count = decay_log.shape
    running = jnp.zeros((head_count, DH, DH), jnp.float32)
    carried = jnp.ones((head_count,), jnp.float32)
    previous = doc_before
    row_order = jnp.arange(BLK, dtype=jnp.int32)
    page_last = (jnp.arange(BLK // PAGE, dtype=jnp.int32) + 1) * PAGE - 1
    outputs, weights, states_all, weights_end = ([], [], [], [])
    for block_id in range(row_count // BLK):
        row_span = slice(block_id * BLK, (block_id + 1) * BLK)
        q_block = queries[row_span]
        k_block = key_rows[row_span]
        v_block = value_rows[row_span]
        doc_block = doc_ids[row_span]
        cumulative = jnp.cumsum(decay_log[row_span], axis=0)
        causal = (row_order[:, None] >= row_order[None, :]) & (
            doc_block[:, None] == doc_block[None, :]
        )
        spread = cumulative.T[:, :, None] - cumulative.T[:, None, :]
        decay_grid = jnp.where(causal[None], jnp.exp(jnp.minimum(spread, 0.0)), 0.0)
        scores = jnp.einsum("thd,shd->hts", q_block, k_block, preferred_element_type=jnp.float32)
        weights_grid = (scores * decay_grid).astype(jnp.bfloat16)
        intra_out = jnp.einsum(
            "hts,shd->thd", weights_grid, v_block, preferred_element_type=jnp.float32
        )
        weight = jnp.exp(cumulative) * (doc_block == previous).astype(jnp.float32)[:, None]
        inter_out = jnp.einsum(
            "thd,hde->the",
            q_block.astype(jnp.float32) * weight[:, :, None],
            running,
            precision=highest,
        )
        outputs.append(intra_out + inter_out)
        weights.append(weight * carried[None, :])
        cumulative_end = cumulative[PAGE - 1 :: PAGE]
        doc_end = doc_block[PAGE - 1 :: PAGE]
        weight_end = weight[PAGE - 1 :: PAGE]
        page_mask = (row_order[None, :] <= page_last[:, None]) & (
            doc_block[None, :] == doc_end[:, None]
        )
        factor = jnp.where(
            page_mask[:, :, None],
            jnp.exp(jnp.minimum(cumulative_end[:, None, :] - cumulative[None, :, :], 0.0)),
            0.0,
        )
        decayed = (k_block[None].astype(jnp.float32) * factor[:, :, :, None]).astype(jnp.bfloat16)
        states = weight_end[:, :, None, None] * running[None] + jnp.einsum(
            "eshd,shf->ehdf", decayed, v_block, preferred_element_type=jnp.float32
        )
        states_all.append(states)
        weights_end.append(weight_end * carried[None, :])
        running = states[-1]
        carried = carried * weight[-1]
        previous = doc_block[-1]
    return (
        jnp.concatenate(outputs),
        jnp.concatenate(weights),
        jnp.concatenate(states_all),
        jnp.concatenate(weights_end),
        carried,
        running,
    )


def partial_softmax(queries, key_rows, value_rows, key_docs):
    samples, doc_count, step_count, features = queries.shape
    row_count = key_rows.shape[0]
    kv_local = key_rows.shape[1] // DH
    group = features // DH // kv_local
    grouped = queries.reshape(samples, doc_count, step_count, kv_local, group, DH)
    scores = jnp.einsum(
        "rpjxgd,nxd->xrpjgn",
        grouped,
        key_rows.reshape(row_count, kv_local, DH),
        preferred_element_type=jnp.float32,
    ) * DH ** (-0.5)
    doc_mask = (key_docs[None, :] == jnp.arange(doc_count, dtype=jnp.int32)[:, None])[
        None, None, :, None, None, :
    ]
    running_max = jnp.max(jnp.where(doc_mask, scores, mask_low), axis=-1)
    weights_grid = jnp.where(doc_mask, jnp.exp(scores - running_max[..., None]), 0.0)
    summed = jnp.einsum(
        "xrpjgn,nxd->xrpjgd",
        weights_grid.astype(jnp.bfloat16),
        value_rows.reshape(row_count, kv_local, DH),
        preferred_element_type=jnp.float32,
    )
    return (running_max, jnp.sum(weights_grid, axis=-1), summed)


def finish_softmax(running_max, denominator, summed, soft_query, soft_key, soft_value):
    samples, doc_count, step_count, features = soft_query.shape
    kv_local = soft_key.shape[3] // DH
    group = features // DH // kv_local
    grouped = soft_query.reshape(samples, doc_count, step_count, kv_local, group, DH)
    own = jnp.einsum(
        "rpjxgd,rpixd->xrpjgi",
        grouped,
        soft_key.reshape(samples, doc_count, step_count, kv_local, DH),
        preferred_element_type=jnp.float32,
    ) * DH ** (-0.5)
    step_mask = (jnp.arange(step_count)[:, None] >= jnp.arange(step_count)[None, :])[
        None, None, None, :, None, :
    ]
    peak = jnp.maximum(running_max, jnp.max(jnp.where(step_mask, own, mask_low), axis=-1))
    rescale = jnp.exp(running_max - peak)
    own_weights = jnp.where(step_mask, jnp.exp(own - peak[..., None]), 0.0)
    numer = summed * rescale[..., None] + jnp.einsum(
        "xrpjgi,rpixd->xrpjgd",
        own_weights.astype(jnp.bfloat16),
        soft_value.reshape(samples, doc_count, step_count, kv_local, DH),
        preferred_element_type=jnp.float32,
    )
    denom = denominator * rescale + jnp.sum(own_weights, axis=-1)
    result = numer / denom[..., None]
    return (
        result.transpose(1, 2, 3, 0, 4, 5)
        .reshape(samples, doc_count, step_count, features)
        .astype(jnp.bfloat16)
    )


def per_device(
    light_query,
    light_key,
    light_value,
    log_decay,
    prompt_pages,
    norm_gain,
    cache_keys,
    cache_values,
    step_query,
    step_key,
    step_value,
    step_decay,
    soft_query,
    soft_key,
    soft_value,
):
    row_count, head_count = log_decay.shape
    device_rank = lax.axis_index(("seq", "rep"))
    row_start = device_rank * row_count
    row_index = jnp.arange(row_count, dtype=jnp.int32)
    doc_ids = token_docs(prompt_pages, row_start + row_index)
    doc_before = token_docs(prompt_pages, jnp.reshape(row_start - 1, (1,)))[0]
    queries = light_query.reshape(row_count, head_count, DH)
    outputs, weights, page_states, page_weights, carried, state_end = local_blocks(
        queries,
        light_key.reshape(row_count, head_count, DH),
        light_value.reshape(row_count, head_count, DH),
        log_decay,
        doc_ids,
        doc_before,
    )
    identity = (jnp.ones((head_count,), jnp.float32), jnp.zeros((head_count, DH, DH), jnp.float32))
    state_in = carried_in((carried, state_end), ("seq", "rep"), join_summaries, identity)[1]
    mixed = outputs + jnp.einsum(
        "thd,hde->the",
        queries.astype(jnp.float32) * weights[:, :, None],
        state_in,
        precision=highest,
    )
    squares = lax.psum(jnp.sum(mixed * mixed, axis=(1, 2)), "tp")
    feature_count = lax.axis_size("tp") * head_count * DH
    light_out = (
        mixed.reshape(row_count, head_count * DH)
        * lax.rsqrt(squares / feature_count + norm_eps)[:, None]
        * norm_gain[None, :]
    ).astype(jnp.bfloat16)
    page_ends = PAGE * jnp.cumsum(prompt_pages)
    page_rows = row_start + (jnp.arange(row_count // PAGE, dtype=jnp.int32) + 1) * PAGE
    true_states = page_states + page_weights[:, :, None, None] * state_in[None]
    owner_map = (page_ends[:, None] == page_rows[None, :]).astype(jnp.float32)
    state_terms = jnp.einsum("pe,ehdf->phdf", owner_map, true_states, precision=highest)
    doc_count = step_query.shape[1]
    step_count = step_query.shape[2]
    share_width = DH // lax.axis_size("seq")
    column_start = lax.axis_index("seq") * share_width
    step_q = step_query[0].reshape(doc_count, step_count, head_count, DH).astype(jnp.float32)
    step_k = step_key[0].reshape(doc_count, step_count, head_count, DH).astype(jnp.float32)
    step_v = step_value[0].reshape(doc_count, step_count, head_count, DH).astype(jnp.float32)
    value_share = lax.dynamic_slice_in_dim(step_v, column_start, share_width, 3)
    final_states = lax.psum(state_terms.astype(jnp.bfloat16), ("seq", "rep")).astype(jnp.float32)
    state_share = lax.dynamic_slice_in_dim(final_states, column_start, share_width, 3)
    decoded_share = decode_steps(state_share, step_q, step_k, value_share, step_decay[0])
    decode_squares = lax.psum(jnp.sum(decoded_share * decoded_share, axis=(2, 3)), ("seq", "tp"))
    gain_share = lax.dynamic_slice_in_dim(
        norm_gain.reshape(head_count, DH), column_start, share_width, 1
    )
    light_decode = (
        decoded_share
        * lax.rsqrt(decode_squares / feature_count + norm_eps)[:, :, None, None]
        * gain_share
    ).astype(jnp.bfloat16)[None]
    other_keys, other_values = from_partner((cache_keys, cache_values), "rep", 0)
    partner_docs = token_docs(prompt_pages, jnp.bitwise_xor(device_rank, 1) * row_count + row_index)
    running_max, denominator, summed = partial_softmax(
        soft_query,
        jnp.concatenate([cache_keys, other_keys]),
        jnp.concatenate([cache_values, other_values]),
        jnp.concatenate([doc_ids, partner_docs]),
    )
    running_max, denominator, summed = combined_all(
        (running_max, denominator, summed), "seq", combine_partials
    )
    soft_decode = finish_softmax(running_max, denominator, summed, soft_query, soft_key, soft_value)
    return (light_out, light_decode, soft_decode)


def solution(mesh):
    in_specs = (
        P(("seq", "rep"), "tp"),
        P(("seq", "rep"), "tp"),
        P(("seq", "rep"), "tp"),
        P(("seq", "rep"), "tp"),
        P(),
        P("tp"),
        P(("seq", "rep"), "tp"),
        P(("seq", "rep"), "tp"),
        P("rep", None, None, "tp"),
        P("rep", None, None, "tp"),
        P("rep", None, None, "tp"),
        P("rep", None, None, "tp"),
        P("rep", None, None, "tp"),
        P("rep", None, None, "tp"),
        P("rep", None, None, "tp"),
    )
    out_specs = (
        P(("seq", "rep"), "tp"),
        P("rep", None, None, "tp", "seq"),
        P("rep", None, None, "tp"),
    )
    return jax.shard_map(
        per_device, mesh=mesh, in_specs=in_specs, out_specs=out_specs, check_vma=False
    )
```

profile of v0, /device:TPU:0, one launch (start us, length us, event | category | flops | bytes accessed | tf_op | source)
XLA Modules:
  0.0 736.3 jit_solution(15273425228899284282)
XLA Ops:
  11.2 1.1 reduce-window.19
  12.5 1.1 reduce-window.21
  13.8 1.9 fusion.113
  16.0 1.1 fusion.112
  17.2 1.3 compare_convert_fusion
  19.0 1.4 select_reduce_fusion
  20.4 1.0 copy-done.16
  21.4 2.0 fusion.61
  23.6 1.3 copy.303
  25.2 1.5 copy.302
  26.7 1.7 convert_element_type.144
  28.4 1.4 copy.301
  31.3 2.1 fusion.51
  34.3 1.0 copy-done.3
  36.9 1.5 fusion.111
  39.7 20.0 %all-gather.3 = bf16[32,1,8]{2,1,0:T(2,128)(2,1)S(1)} all-gather(bf16[1,1,8]{2,1,0:T(2,128)(2,1)S(1)} %bitcast.341), channel_id=1, replica_groups=mesh['seq'=16,'tp'=8,'rep'=2] {'seq','rep'}, dimensions={0}, use_global_device_ids=true | all-gather | bytes 528 | tf_op jit(solution)/shard_map/all_gather | solution.py:19
  60.3 2.3 copy.305
  62.7 1.8 copy.304
  64.4 1.4 copy.298
  70.7 1.5 select_reduce_fusion.1
  72.1 1.0 fusion.57
  74.0 2.6 fusion.73
  76.6 6.3 fusion.9
  82.9 6.9 bitcast_add_fusion.5
  89.8 6.3 fusion.10
  96.0 6.9 bitcast_add_fusion.4
  103.0 22.7 %all-gather = f32[64,4,8]{2,1,0:T(4,128)S(1)} all-gather(f32[4,4,8]{2,1,0:T(4,128)S(1)} %get-tuple-element.391), channel_id=2, replica_groups=mesh['seq'=16,'tp'=8,'rep'=2] {'seq'}, dimensions={0}, use_global_device_ids=true | all-gather | bytes 8704 | tf_op jit(solution)/shard_map/all_gather | solution.py:41
  126.1 22.0 %all-gather.1 = f32[64,4,8]{2,1,0:T(4,128)S(1)} all-gather(f32[4,4,8]{2,1,0:T(4,128)S(1)} %fusion.60), channel_id=3, replica_groups=mesh['seq'=16,'tp'=8,'rep'=2] {'seq'}, dimensions={0}, use_global_device_ids=true | all-gather | bytes 8704 | tf_op jit(solution)/shard_map/all_gather | solution.py:41
  148.9 15.7 %while.32 = (s32[]{:T(128)}, f32[1,1,4,4,8]{4,3,2,1,0:T(4,128)S(1)}, f32[1,1,4,4,8]{4,3,2,1,0:T(4,128)S(1)}, f32[1,1,4,4,8,128]{5,4,3,2,1,0:T(8,128)S(1)}, f32[1...) while((s32[]{:T(128)}, ...), condition=%wide.region_18.19_spmd, body=%wide.region_17.18_spmd.sunk | while | flops 50053 | bytes 204443 | solution.py:46
  149.0 1.0 fusion.131
  151.1 1.0 fusion.131
  152.1 1.0 fusion.131
  154.2 1.0 fusion.131
  155.3 1.0 fusion.131
  157.4 1.0 fusion.131
  165.8 7.8 %multiply_reduce_fusion = (f32[1024]{0:T(1024)S(1)}, f32[1024,8,128]{2,0,1:T(8,128)}) fusion(f32[8,128,128]{2,1,0:T(8,128)S(1)} %get-tuple-element.225, f32[1024,8]{0,1:T(8,128)S(1)} %pad_maximum_fusion, f32[512,8,128]{2,0,1:T(8,128)} %bitcast_add_fusion.4, f32[512,8,128]{2,0,1:T(8,128)} %bitcast_add_fusion.5, bf16[1024,1024]{1,0:T(8,128)(2,1)} %param.19), kind=kOutput, calls=%fused_computation.22 | convolution fusion | flops 1616903168 | bytes 11046912 | tf_op jit(solution)/shard_map/thd,hde->the/dot_general | solution.py:237
  173.6 5.5 copy.241
  179.1 20.2 %psum.21 = f32[1024]{0:T(1024)S(1)} all-reduce(f32[1024]{0:T(1024)S(1)} %get-tuple-element.389), channel_id=1, replica_groups=mesh['seq'=16,'tp'=8,'rep'=2] {'tp'}, use_global_device_ids=true, to_apply=%region_10.11 | all-reduce | flops 1024 | bytes 8192 | tf_op jit(solution)/shard_map/psum | solution.py:243
  199.9 4.3 fusion.45
  204.3 2.6 fusion.8
  207.0 2.8 copy.259
  209.7 158.9 %all-reduce.2.cloned.1.call-done = bf16[4,8,128,128]{3,0,2,1:T(4,128)(2,1)} async-done(((bf16[4,8,128,128]{3,0,2,1:T(4,128)(2,1)}), bf16[4,8,128,128]{3,0,2,1:T(4,128)(2,1)}) %all-reduce.2.cloned.1.call-update) | async-done | bytes 1048592 | tf_op jit(solution)/shard_map/psum | solution.py:263
  368.7 7.7 %bitcast_add_fusion = (f32[4,8,128,8]{3,0,2,1:T(4,128)S(1)}, f32[4,8,128,8]{3,0,2,1:T(4,128)S(1)}, f32[4,8,128,8]{3,0,2,1:T(4,128)S(1)}, f32[4,8,128,8]{3,0,2,1:T(4,128)S(1)}) fusion(f32[4,8,128]{0,2,1:T(8,128)S(1)} %copy-done.15, f32[4,8,8]{2,0,1:T(4,128)S(1)} %get-tuple-element.397, f32[4,8]{0,1:T(8,128)S(1)} %copy-done.31, ...), kind=kLoop, calls=%fused_computation.36 | loop fusion | flops 425984 | bytes 659972 | tf_op jit(solution)/shard_map/add | solution.py:74
  376.4 1.1 fusion.20
  377.5 1.1 fusion.22
  378.6 1.1 fusion.24
  379.6 1.1 fusion.26
  380.8 347.9 %psum.23 = f32[4,4]{0,1:T(4,128)S(1)} all-reduce(f32[4,4]{0,1:T(4,128)S(1)} %fusion.77), channel_id=1, replica_groups=mesh['seq'=16,'tp'=8,'rep'=2] {'seq','tp'}, use_global_device_ids=true, to_apply=%region_13.14 | all-reduce | flops 16 | bytes 128 | tf_op jit(solution)/shard_map/psum | solution.py:266
  (226 shorter events, 30.5 us)
Async XLA Ops:
  7.2 157.6 %copy-start = (bf16[1,4,4,128]{3,2,1,0:T(4,128)(2,1)S(1)}, bf16[1,4,4,128]{3,2,1,0:T(4,128)(2,1)}, u32[]{:S(2)}) copy-start(bf16[1,4,4,128]{3,2,1,0:T(4,128)(2,1)} %param.33) | copy-start | bytes 12292
  7.2 140.9 %all-gather.9.cloned.1.call-start = ((), (), s32[]{:S(2)}) async-start(), calls=%async_computation.2 | async-start | bytes 1114112 | tf_op jit(solution)/shard_map/all_gather | solution.py:41
  7.2 11.7 %collective-permute-start = (bf16[1024,128]{1,0:T(8,128)(2,1)}, bf16[1024,128]{1,0:T(8,128)(2,1)}, u32[]{:S(2)}, u32[]{:S(2)}) collective-permute-start(bf16[1024,128]{1,0:T(8,128)(2,1)} %param.25), channel_id=1, source_target_pairs={{0,1},{1,0},{2,3},{3,2},{4,5},{5,4},{6,7},{7,6},{8,9},{9,8},{10,11... | collective-permute-start | bytes 786440 | tf_op jit(solution)/shard_map/ppermute | solution.py:37
  7.3 13.1 %collective-permute-start.1 = (bf16[1024,128]{1,0:T(8,128)(2,1)}, bf16[1024,128]{1,0:T(8,128)(2,1)}, u32[]{:S(2)}, u32[]{:S(2)}) collective-permute-start(bf16[1024,128]{1,0:T(8,128)(2,1)} %param.26), channel_id=1, source_target_pairs={{0,1},{1,0},{2,3},{3,2},{4,5},{5,4},{6,7},{7,6},{8,9},{9,8},{10,11... | collective-permute-start | bytes 786440 | tf_op jit(solution)/shard_map/ppermute | solution.py:37
  13.8 2.2 copy-start.13
  16.0 2.9 copy-start.25
  17.2 6.3 copy-start.20
  20.4 1.0 copy-start.16
  23.5 142.3 %all-gather.7.cloned.1.call-start = ((), (), s32[]{:S(2)}) async-start(), calls=%async_computation | async-start | bytes 8650752 | tf_op jit(solution)/shard_map/all_gather | solution.py:19
  23.5 7.2 copy-start.22
  26.7 3.0 copy-start.5
  30.3 1.0 copy-start.8
  31.3 2.2 copy-start.2
  31.3 2.2 copy-start.10
  33.5 3.4 copy-start.1
  34.3 1.0 copy-start.3
  36.1 332.6 %all-reduce.2.cloned.1.call-start = ((), (), s32[]{:S(2)}) async-start(), calls=%async_computation.1 | async-start | bytes 2097152 | tf_op jit(solution)/shard_map/psum | solution.py:263
  36.9 1.5 copy-start.37
  36.9 2.2 copy-start.29
  38.4 24.3 %copy-start.12 = (bf16[512,1024]{1,0:T(8,128)(2,1)S(1)}, bf16[512,1024]{1,0:T(8,128)(2,1)}, u32[]{:S(2)}) copy-start(bf16[512,1024]{1,0:T(8,128)(2,1)} %get-tuple-element.354) | copy-start | bytes 3145732
  39.7 30.9 %copy-start.41 = (pred[4,4]{1,0:T(4,128)(4,1)}, pred[4,4]{1,0:T(4,128)(4,1)S(1)}, u32[]{:S(2)}) copy-start(pred[4,4]{1,0:T(4,128)(4,1)S(1)} %iota_compare_fusion.3) | copy-start | bytes 52
  60.3 4.1 copy-start.23
  62.6 3.2 copy-start.26
  62.6 5.9 copy-start.27
  62.6 8.0 %copy-start.43 = (bf16[1,4,4,128]{3,2,1,0:T(4,128)(2,1)S(1)}, bf16[1,4,4,128]{3,2,1,0:T(4,128)(2,1)}, u32[]{:S(2)}) copy-start(bf16[1,4,4,128]{3,2,1,0:T(4,128)(2,1)} %param.32) | copy-start | bytes 12292
  68.6 8.0 %copy-start.7 = (bf16[512,1024]{0,1:T(8,128)(2,1)S(1)}, bf16[512,1024]{0,1:T(8,128)(2,1)}, u32[]{:S(2)}) copy-start(bf16[512,1024]{0,1:T(8,128)(2,1)} %copy.301) | copy-start | bytes 3145732
  68.6 8.0 %copy-start.9 = (bf16[512,1024]{0,1:T(8,128)(2,1)S(1)}, bf16[512,1024]{0,1:T(8,128)(2,1)}, u32[]{:S(2)}) copy-start(bf16[512,1024]{0,1:T(8,128)(2,1)} %copy-done.8) | copy-start | bytes 3145732
  82.9 6.9 copy-start.6
  82.9 6.9 copy-start.11
  96.0 29.7 %copy-start.17 = (f32[4,4,8,2048]{3,2,1,0:T(8,128)S(1)}, f32[4,4,8,2048]{3,2,1,0:T(8,128)}, u32[]{:S(2)}) copy-start(f32[4,4,8,2048]{3,2,1,0:T(8,128)} %copy-done.16) | copy-start | bytes 3145732
  96.0 29.7 %copy-start.21 = (pred[4,2048]{1,0:T(4,128)(4,1)S(1)}, pred[4,2048]{1,0:T(4,128)(4,1)}, u32[]{:S(2)}) copy-start(pred[4,2048]{1,0:T(4,128)(4,1)} %copy-done.20) | copy-start | bytes 24580
  103.0 61.7 %copy-start.28 = (f32[4,4,8]{2,1,0:T(4,128)S(1)}, f32[4,4,8]{2,1,0:T(4,128)}, u32[]{:S(2)}) copy-start(f32[4,4,8]{2,1,0:T(4,128)} %get-tuple-element.393) | copy-start | bytes 1540
  103.0 61.7 %copy-start.24 = (f32[4,4,8,4]{2,3,1,0:T(4,128)S(1)}, f32[4,4,8,4]{2,3,1,0:T(4,128)}, u32[]{:S(2)}) copy-start(f32[4,4,8,4]{2,3,1,0:T(4,128)} %get-tuple-element.394) | copy-start | bytes 6148
  103.0 61.7 %copy-start.42 = (pred[4,4]{1,0:T(4,128)(4,1)S(1)}, pred[4,4]{1,0:T(4,128)(4,1)}, u32[]{:S(2)}) copy-start(pred[4,4]{1,0:T(4,128)(4,1)} %copy-done.41) | copy-start | bytes 52
  173.6 25.6 %copy-start.4 = (f32[2,8,128,128]{3,2,0,1:T(8,128)S(1)}, f32[2,8,128,128]{3,2,0,1:T(8,128)}, u32[]{:S(2)}) copy-start(f32[2,8,128,128]{3,2,0,1:T(8,128)} %copy-done.3) | copy-start | bytes 3145732
  173.6 25.6 %copy-start.36 = (f32[4,8]{0,1:T(8,128)S(1)}, f32[4,8]{0,1:T(8,128)}, u32[]{:S(2)}) copy-start(f32[4,8]{0,1:T(8,128)} %pad_maximum_fusion.1) | copy-start | bytes 388
  199.2 0.7 copy-start.39
  199.2 0.7 copy-start.40
  199.9 4.4 copy-start.30
  206.9 161.8 %copy-start.14 = (f32[4,8,128]{0,2,1:T(8,128)S(1)}, f32[4,8,128]{0,2,1:T(8,128)}, u32[]{:S(2)}) copy-start(f32[4,8,128]{0,2,1:T(8,128)} %get-tuple-element.361) | copy-start | bytes 49156
  206.9 161.8 %copy-start.15 = (f32[4,8,128]{0,2,1:T(8,128)S(1)}, f32[4,8,128]{0,2,1:T(8,128)}, u32[]{:S(2)}) copy-start(f32[4,8,128]{0,2,1:T(8,128)} %get-tuple-element.362) | copy-start | bytes 49156
  206.9 161.8 %copy-start.18 = (f32[4,8,8]{2,0,1:T(4,128)S(1)}, f32[4,8,8]{2,0,1:T(4,128)}, u32[]{:S(2)}) copy-start(f32[4,8,8]{2,0,1:T(4,128)} %get-tuple-element.399) | copy-start | bytes 3076
  206.9 161.8 %copy-start.19 = (f32[4,8,8]{2,0,1:T(4,128)S(1)}, f32[4,8,8]{2,0,1:T(4,128)}, u32[]{:S(2)}) copy-start(f32[4,8,8]{2,0,1:T(4,128)} %get-tuple-element.400) | copy-start | bytes 3076
  206.9 161.8 %copy-start.31 = (f32[4,8]{0,1:T(8,128)S(1)}, f32[4,8]{0,1:T(8,128)}, u32[]{:S(2)}) copy-start(f32[4,8]{0,1:T(8,128)} %copy.250) | copy-start | bytes 388
  206.9 161.8 %copy-start.32 = (f32[4,8]{0,1:T(8,128)S(1)}, f32[4,8]{0,1:T(8,128)}, u32[]{:S(2)}) copy-start(f32[4,8]{0,1:T(8,128)} %copy.248) | copy-start | bytes 388
  206.9 161.8 %copy-start.33 = (f32[4,8]{0,1:T(8,128)S(1)}, f32[4,8]{0,1:T(8,128)}, u32[]{:S(2)}) copy-start(f32[4,8]{0,1:T(8,128)} %copy.242) | copy-start | bytes 388
  206.9 161.8 %copy-start.34 = (f32[4,8]{0,1:T(8,128)S(1)}, f32[4,8]{0,1:T(8,128)}, u32[]{:S(2)}) copy-start(f32[4,8]{0,1:T(8,128)} %copy.246) | copy-start | bytes 388
  378.6 350.3 %copy-start.35 = (f32[8,8]{1,0:T(8,128)S(1)}, f32[8,8]{1,0:T(8,128)}, u32[]{:S(2)}) copy-start(f32[8,8]{1,0:T(8,128)} %constant_dynamic-slice_fusion.3) | copy-start | bytes 772
  (1 other events, 0.6 us)
Sparse Core Ops, SparseCore 0:
  23.6 48.9 all-gather.8
  75.2 57.8 all-gather.6
  204.4 164.2 all-reduce.1
where the time goes:
time: 745 us; the launch traced here: 736 us
  blocking collectives  433 us (58%)
  waiting for transfers between devices  159 us (21%)
  matrix products  50.9 us (7%)
  other arithmetic  42.3 us (6%)
  local copies, waits for them, and re-layouts  35.4 us (5%)
  between operations  14.6 us (2%)
    psum x1, blocking collectives, per_device(): lax.psum(jnp.sum(decoded_share * decoded_share, axis=(2, 3)), ('seq', 'tp'))  348 us
    psum x1, waiting for transfers between devices, per_device(): lax.psum(state_terms.astype(jnp.bfloat16), ('seq', 'rep'))  159 us
    all_gather x2, blocking collectives, combined_all(): gathered = jax.tree.map(lambda a: lax.all_gather(a, axis), part)  44.7 us
    psum x1, blocking collectives, per_device(): squares = lax.psum(jnp.sum(mixed * mixed, axis=(1, 2)), 'tp')  20.2 us
    all_gather x1, blocking collectives, carried_in(): lax.all_gather(a.astype(kind), axis)  20 us
    unnamed x95, local copies, waits for them, and re-layouts  15.2 us
  transfers between devices with their start and end apart: 5, of which 1 were waited for; matrix products, arithmetic and copies ran while one was open for 13% of the time, Pallas kernels for 0%

commit v1 on v0

v1 whole, which is shorter than its diff:
```python
import math

import jax
import jax.numpy as jnp
from jax import lax
from jax.experimental import pallas as pl
from jax.experimental.pallas import tpu as pltpu
from jax.sharding import PartitionSpec as P

DH = 128
PAGE = 256
DOCS = 4
STEPS = 4
HEADS = 8
SEQ = 16
TP = 8
ROWS = 1024
PAGES_DEV = ROWS // PAGE
HALF = HEADS // 2 * 8

norm_eps = 1e-06
mask_low = -1e30
LOG2E = math.log2(math.e)
highest = lax.Precision.HIGHEST
f32 = jnp.float32
bf16 = jnp.bfloat16
MESH = pl.DeviceIdType.MESH

NN = (((1,), (0,)), ((), ()))
NT = (((1,), (1,)), ((), ()))
TN = (((0,), (0,)), ((), ()))

P_KEYS, P_VALUES, P_STATE, P_WEIGHT, P_SLOTS, P_CARRY, P_FINAL = range(7)
S_STATE, S_SLOTS, S_SOFT, S_BACK, S_GATHER = range(5)


def mm(a, b, dims, precision=None):
    return lax.dot_general(a, b, dims, precision=precision, preferred_element_type=f32)


def head_cols(h):
    return slice(h * DH, (h + 1) * DH)


def expand(rows):
    return jnp.concatenate(
        [jnp.broadcast_to(rows[i : i + 1], (8, DH)) for i in range(HEADS // 2)], axis=0
    )


def kernel(
    pages_ref, q_ref, k_ref, v_ref, g_ref, gain_ref, ck_ref, cv_ref,
    stq_ref, stk_ref, stv_ref, std_ref, sfq_ref, sfk_ref, sfv_ref,
    out_ref, dec_ref, soft_ref,
    mixed, ccol, crow, states, before, weights, stq, stk, stv, std, sfq, sfk, sfv,
    other_k, other_v,
    pair_state, pair_state_in, pair_weight, pair_weight_in, pair_slots, pair_slots_in,
    send_state, recv_state, send_slots, recv_slots, send_soft, recv_soft,
    carry, send_back, recv_back, pair_carry, pair_carry_in, carry_all,
    pair_final, pair_final_in, final_all, dec_own, send_gather, recv_gather, recv_tp,
    pair_send, pair_recv, seq_send, seq_recv, tp_send, tp_recv,
):
    me = lax.axis_index("seq")
    tp = lax.axis_index("tp")
    rep = lax.axis_index("rep")
    first_core = rep == 0
    own_rows = pl.ds(pl.multiple_of(rep * HALF, HALF), HALF)
    other_rows = pl.ds(pl.multiple_of((1 - rep) * HALF, HALF), HALF)

    def pair_copy(which, src, dst):
        return pltpu.make_async_remote_copy(
            src_ref=src, dst_ref=dst, send_sem=pair_send.at[which], recv_sem=pair_recv.at[which],
            device_id=(me, tp, 1 - rep), device_id_type=MESH,
        )

    def seq_copy(phase, src, dst, hop):
        target = lax.rem(me + hop, SEQ)
        return pltpu.make_async_remote_copy(
            src_ref=src(target), dst_ref=dst.at[me],
            send_sem=seq_send.at[phase, hop], recv_sem=seq_recv.at[phase, hop],
            device_id=(target, tp, rep), device_id_type=MESH,
        )

    def seq_start(phase, src, dst):
        def one(hop, _):
            seq_copy(phase, src, dst, hop).start()
            return 0

        lax.fori_loop(1, SEQ, one, 0)

    def seq_wait(phase, src, dst):
        def one(hop, _):
            source = lax.rem(me + SEQ - hop, SEQ)
            pltpu.make_async_remote_copy(
                src_ref=src(source), dst_ref=dst.at[source],
                send_sem=seq_send.at[phase, hop], recv_sem=seq_recv.at[phase, hop],
                device_id=(source, tp, rep), device_id_type=MESH,
            ).wait_recv()
            return 0

        lax.fori_loop(1, SEQ, one, 0)

    def seq_sent(phase, src, dst):
        def one(hop, _):
            seq_copy(phase, src, dst, hop).wait_send()
            return 0

        lax.fori_loop(1, SEQ, one, 0)

    src_state = lambda t: send_state.at[t]
    src_slots = lambda t: send_slots.at[t]
    src_soft = lambda t: send_soft.at[t]
    src_back = lambda t: send_back.at[t]
    src_gather = lambda t: send_gather

    def tp_copy(hop):
        return pltpu.make_async_remote_copy(
            src_ref=send_gather, dst_ref=recv_tp.at[tp],
            send_sem=tp_send.at[hop], recv_sem=tp_recv.at[hop],
            device_id=(me, lax.rem(tp + hop, TP), rep), device_id_type=MESH,
        )

    barrier = pltpu.get_barrier_semaphore()

    def greet_seq(hop, _):
        pl.semaphore_signal(
            barrier, inc=1, device_id=(lax.rem(me + hop, SEQ), tp, rep), device_id_type=MESH
        )
        return 0

    def greet_tp(hop, _):
        pl.semaphore_signal(
            barrier, inc=1, device_id=(me, lax.rem(tp + hop, TP), rep), device_id_type=MESH
        )
        return 0

    lax.fori_loop(1, SEQ, greet_seq, 0)
    lax.fori_loop(1, TP, greet_tp, 0)
    pl.semaphore_signal(barrier, inc=1, device_id=(me, tp, 1 - rep), device_id_type=MESH)

    ends = []
    for p in range(DOCS):
        ends.append(pages_ref[p] + (ends[-1] if ends else 0))
    chip_page = me * (2 * PAGES_DEV)
    dev_page = chip_page + rep * PAGES_DEV

    def flag(cond):
        return jnp.where(cond, 1, 0).astype(jnp.int32)

    def goes_on(page):
        hits = sum(flag(e == page) for e in ends)
        return jnp.where(hits == 0, 1.0, 0.0).astype(f32)

    def doc_of(page):
        return sum((e <= page).astype(jnp.int32) for e in ends)

    slot_page, slot_valid = [], []
    inside = [flag(jnp.logical_and(e > chip_page, e < chip_page + 2 * PAGES_DEV)) for e in ends]
    for s in range(2):
        place = 0
        for p in range(DOCS):
            rank = sum(inside[:p]) if p else 0
            place = place + inside[p] * flag(rank == s) * (ends[p] - chip_page)
        local = place - 1 - rep * PAGES_DEV
        ok = jnp.logical_and(
            place > 0, jnp.logical_and(local >= 0, local < PAGES_DEV)
        )
        slot_page.append(jnp.clip(local, 0, PAGES_DEV - 1))
        slot_valid.append(jnp.where(ok, 1.0, 0.0).astype(f32))

    rows_i = lax.broadcasted_iota(jnp.int32, (PAGE, PAGE), 0)
    cols_i = lax.broadcasted_iota(jnp.int32, (PAGE, PAGE), 1)
    states[0] = jnp.zeros((SEQ, 2 * HALF, DH), f32)

    def state_page(k, carried):
        rows = pl.ds(pl.multiple_of(k * PAGE, PAGE), PAGE)
        g = g_ref[rows, :] * LOG2E
        lower = (rows_i >= cols_i).astype(f32)
        upper = (rows_i <= cols_i).astype(f32)
        c = mm(lower, g, NN, highest)
        ccol[rows, :] = c
        crow[k] = mm(g, upper, TN, highest)
        decay = jnp.exp2(mm(g, jnp.ones((PAGE, DH), f32), TN, highest))
        cont = goes_on(dev_page + k)
        before[k] = carried * cont
        keep = decay * cont
        after = carried * keep
        weights[k] = after
        fade = jnp.exp2(c[PAGE - 1 : PAGE, :] - c)
        for h in range(HEADS):
            kd = (k_ref[rows, head_cols(h)].astype(f32) * fade[:, h : h + 1]).astype(bf16)
            add = mm(v_ref[rows, head_cols(h)], kd, TN)
            old = states[k, :, h * 8 : h * 8 + 8, :]
            states[k + 1, :, h * 8 : h * 8 + 8, :] = old * keep[h : h + 1, :][None] + add.reshape(
                SEQ, 8, DH
            )
        return after

    total = lax.fori_loop(0, PAGES_DEV, state_page, jnp.ones((HEADS, DH), f32))

    pl.semaphore_wait(barrier, SEQ - 1 + TP - 1 + 1)
    pair_state[...] = states[PAGES_DEV, :, other_rows, :].astype(bf16)
    pair_weight[0:8] = total
    for s in range(2):
        w = jnp.zeros((HEADS, DH), f32)
        for k in range(PAGES_DEV):
            pick = jnp.where(slot_page[s] == k, slot_valid[s], 0.0).astype(f32)
            w = w + pick * weights[k]
        pair_weight[8 + 8 * s : 16 + 8 * s] = w
    pair_copy(P_STATE, pair_state, pair_state_in).start()
    pair_copy(P_WEIGHT, pair_weight, pair_weight_in).start()
    for s in range(2):
        pair_slots[s] = (states[slot_page[s] + 1][:, 0:HALF, :] * slot_valid[s]).astype(bf16)
        pair_slots[2 + s] = (states[slot_page[s] + 1][:, HALF:, :] * slot_valid[s]).astype(bf16)
    pair_other = pair_slots.at[pl.ds((1 - rep) * 2, 2)]
    pair_copy(P_SLOTS, pair_other, pair_slots_in).start()
    pair_copy(P_KEYS, ck_ref, other_k).start()
    pair_copy(P_VALUES, cv_ref, other_v).start()

    causal = rows_i >= cols_i

    def inside_page(k):
        rows = pl.ds(pl.multiple_of(k * PAGE, PAGE), PAGE)
        c = ccol[rows, :]
        r = crow[k]
        for h in range(HEADS):
            scores = mm(q_ref[rows, head_cols(h)], k_ref[rows, head_cols(h)], NT)
            grid = jnp.exp2(c[:, h : h + 1] - r[h : h + 1, :])
            block = jnp.where(causal, scores * grid, 0.0).astype(bf16)
            mixed[rows, head_cols(h)] = mm(block, v_ref[rows, head_cols(h)], NN)

    def inside_loop(first, last):
        def one(k, _):
            inside_page(k)
            return 0

        lax.fori_loop(first, last, one, 0)

    inside_loop(0, 1)

    def half(x):
        return lax.select(first_core, x[0:4], x[4:8])

    pair_copy(P_STATE, pair_state, pair_state_in).wait_recv()
    pair_copy(P_WEIGHT, pair_weight, pair_weight_in).wait_recv()
    own_state = states[PAGES_DEV, :, own_rows, :]
    got_state = pair_state_in[...].astype(f32)
    state0 = lax.select(first_core, own_state, got_state)
    state1 = lax.select(first_core, got_state, own_state)
    own_w = [half(pair_weight[8 * n : 8 * n + 8]) for n in range(3)]
    got_w = [half(pair_weight_in[8 * n : 8 * n + 8]) for n in range(3)]
    w0 = [lax.select(first_core, a, b) for a, b in zip(own_w, got_w)]
    w1 = [lax.select(first_core, b, a) for a, b in zip(own_w, got_w)]
    chip_state = expand(w1[0])[None] * state0 + state1
    chip_w = jnp.concatenate([w1[0] * w0[0], w0[1] + w1[1] * w0[0]], axis=0)
    chip_hi = chip_w.astype(bf16).astype(f32)
    chip_rows = jnp.concatenate([chip_hi, chip_w - chip_hi], axis=0).astype(bf16)
    send_state[:, 0:HALF, :] = chip_state.astype(bf16)
    send_state[:, HALF:, :] = jnp.broadcast_to(chip_rows[None], (SEQ, 16, DH))
    seq_start(S_STATE, src_state, recv_state)
    recv_state[me] = send_state[me]

    pair_copy(P_SLOTS, pair_other, pair_slots_in).wait_recv()
    for s in range(2):
        own_slot = states[slot_page[s] + 1][:, 0:HALF, :]
        own_slot = lax.select(first_core, own_slot, states[slot_page[s] + 1][:, HALF:, :])
        slot = own_slot * slot_valid[s] + pair_slots_in[s].astype(f32)
        slot = slot + expand(w1[1 + s])[None] * state0
        send_slots[:, s] = slot.astype(bf16)
    seq_start(S_SLOTS, src_slots, recv_slots)
    recv_slots[me] = send_slots[me]

    for p in range(DOCS):
        part = slice(4 * p, 4 * p + 4)
        stq[part, :] = stq_ref[0, p].astype(f32)
        stk[part, :] = stk_ref[0, p].astype(f32)
        stv[part, :] = stv_ref[0, p].astype(f32)
        std[part, :] = std_ref[0, p]
        sfk[p] = sfk_ref[0, p].astype(f32)
        sfv[p] = sfv_ref[0, p].astype(f32)
        for h in range(HEADS):
            sfq[pl.ds(p * 32 + h, 4, stride=8), :] = sfq_ref[0, p, :, head_cols(h)].astype(f32)

    scale = DH**-0.5 * LOG2E
    pair_copy(P_KEYS, ck_ref, other_k).wait_recv()
    pair_copy(P_VALUES, cv_ref, other_v).wait_recv()
    queries = sfq[...].astype(bf16)
    query_doc = lax.broadcasted_iota(jnp.int32, (DH, ROWS), 0) // 32
    key_page = lax.broadcasted_iota(jnp.int32, (1, ROWS), 1) // PAGE
    score, here = [], []
    for base, key_block in ((dev_page, ck_ref), (chip_page + (1 - rep) * PAGES_DEV, other_k)):
        score.append(mm(queries, key_block[...], NT) * scale)
        here.append(query_doc == jnp.broadcast_to(doc_of(key_page + base), (DH, ROWS)))
    peak = jnp.maximum(
        *[
            jnp.max(jnp.where(m, s, mask_low), axis=1, keepdims=True)
            for m, s in zip(here, score)
        ]
    )
    chance = [jnp.where(m, jnp.exp2(s - peak), 0.0) for m, s in zip(here, score)]
    amount = sum(jnp.sum(x, axis=1, keepdims=True) for x in chance)
    numer = mm(chance[0].astype(bf16), cv_ref[...], NN) + mm(
        chance[1].astype(bf16), other_v[...], NN
    )
    lane = lax.broadcasted_iota(jnp.int32, (DH, DH), 1)
    both = jnp.where(lane < 64, jnp.broadcast_to(peak, (DH, DH)), jnp.broadcast_to(amount, (DH, DH)))
    send_soft[:, 0:8, :] = numer.reshape(SEQ, 8, DH)
    send_soft[:, 8:16, :] = both.reshape(SEQ, 8, DH)
    seq_start(S_SOFT, src_soft, recv_soft)
    recv_soft[me] = send_soft[me]

    seq_wait(S_STATE, src_state, recv_state)
    running = jnp.zeros((HALF, DH), f32)
    for j in range(SEQ):
        carry[j] = running
        send_back[j] = running.astype(bf16)
        rows = recv_state[j, HALF:, :].astype(f32)
        running = expand(rows[0:4] + rows[8:12]) * running + recv_state[j, 0:HALF, :].astype(f32)
    carry[SEQ] = running
    seq_start(S_BACK, src_back, recv_back)
    recv_back[me] = send_back[me]

    inside_loop(1, 3)

    seq_wait(S_SLOTS, src_slots, recv_slots)
    for p in range(DOCS):
        last_page = jnp.clip(ends[p] - 1, 0, 2 * PAGES_DEV * SEQ - 1)
        chip = lax.shift_right_logical(last_page, 3)
        chip_last = jnp.bitwise_and(last_page, 7) == 7
        rank = sum(
            [flag(lax.shift_right_logical(ends[o] - 1, 3) == chip) for o in range(p)],
            jnp.int32(0),
        )
        rows = recv_state[chip][HALF:, :].astype(f32)
        w = expand(rows[4:8] + rows[12:16]) * jnp.where(rank == 0, 1.0, 0.0).astype(f32)
        ended = recv_slots[chip, jnp.minimum(rank, 1)].astype(f32) + w * carry[chip]
        final = lax.select(chip_last, carry[chip + 1], ended)
        final_all[p, own_rows, :] = final
        pair_final[p] = final.astype(bf16)
    pair_copy(P_FINAL, pair_final, pair_final_in).start()

    inside_loop(3, 4)

    seq_wait(S_BACK, src_back, recv_back)
    carry0 = recv_back[...].astype(f32)
    carry1 = expand(w0[0])[None] * carry0 + state0
    carry_all[:, own_rows, :] = lax.select(first_core, carry0, carry1)
    pair_carry[...] = lax.select(first_core, carry1, carry0).astype(bf16)
    pair_copy(P_CARRY, pair_carry, pair_carry_in).start()

    seq_wait(S_SOFT, src_soft, recv_soft)
    doc = me // STEPS
    step = lax.rem(me, STEPS)
    own_q = sfq[pl.ds(pl.multiple_of(me * 8, 8), 8), :]
    own_k = sfk[doc]
    own_v = sfv[doc]
    peaks = [recv_soft[s, 8:16, 0:1] for s in range(SEQ)]
    amounts = [recv_soft[s, 8:16, 64:65] for s in range(SEQ)]
    numers = [recv_soft[s, 0:8, :] for s in range(SEQ)]
    top = peaks[0]
    for x in peaks[1:]:
        top = jnp.maximum(top, x)
    own = []
    for i in range(STEPS):
        s = jnp.sum(own_q * own_k[i : i + 1, :], axis=1, keepdims=True) * scale
        own.append(lax.select(step >= i, s, jnp.full((8, 1), mask_low, f32)))
        top = jnp.maximum(top, own[-1])
    numer = jnp.zeros((8, DH), f32)
    amount = jnp.zeros((8, 1), f32)
    for s in range(SEQ):
        shrink = jnp.exp2(peaks[s] - top)
        numer = numer + numers[s] * shrink
        amount = amount + amounts[s] * shrink
    for i in range(STEPS):
        e = lax.select(step >= i, jnp.exp2(own[i] - top), jnp.zeros((8, 1), f32))
        numer = numer + e.astype(bf16).astype(f32) * own_v[i : i + 1, :]
        amount = amount + e
    send_gather[0:8, :] = numer / amount

    pair_copy(P_FINAL, pair_final, pair_final_in).wait_recv()
    final_all[:, other_rows, :] = pair_final_in[...].astype(f32)
    t16 = lax.broadcasted_iota(jnp.int32, (16, 16), 0)
    s16 = lax.broadcasted_iota(jnp.int32, (16, 16), 1)
    chain = jnp.logical_and(t16 // STEPS == s16 // STEPS, t16 >= s16)
    chain_t = jnp.logical_and(t16 // STEPS == s16 // STEPS, t16 <= s16)
    fall = std[...] * LOG2E
    fall_col = mm(chain.astype(f32), fall, NN, highest)
    fall_row = mm(fall, chain_t.astype(f32), TN, highest)
    f128 = lax.broadcasted_iota(jnp.int32, (DH, 8), 0)
    c128 = lax.broadcasted_iota(jnp.int32, (DH, 8), 1)
    pick = (f128 == c128 + me * 8).astype(f32)
    r32 = lax.broadcasted_iota(jnp.int32, (32, 8), 0)
    c32 = lax.broadcasted_iota(jnp.int32, (32, 8), 1)
    fold = (jnp.bitwise_and(r32, 7) == c32).astype(f32)
    t32 = lax.broadcasted_iota(jnp.int32, (16, 32), 0)
    p32 = lax.broadcasted_iota(jnp.int32, (16, 32), 1)
    same = t32 // STEPS == p32 // 8
    squares = jnp.zeros((16, 8), f32)
    for h in range(HEADS):
        q = stq[:, head_cols(h)]
        k = stk[:, head_cols(h)]
        v = mm(stv[:, head_cols(h)], pick, NN, highest)
        spread = jnp.exp2(fall_col[:, h : h + 1] - fall_row[h : h + 1, :])
        grid = jnp.where(chain, mm(q, k, NT, highest) * spread, 0.0)
        final = final_all[:, h * 8 : h * 8 + 8, :].reshape(32, DH)
        read = jnp.where(same, mm(q, final, NT, highest), 0.0)
        value = mm(read, fold, NN, highest) * jnp.exp2(fall_col[:, h : h + 1])
        value = value + mm(grid, v, NN, highest)
        dec_own[h] = value
        squares = squares + value * value
    send_gather[8:24, :] = mm(squares, jnp.ones((8, DH), f32), NN, highest)
    seq_start(S_GATHER, src_gather, recv_gather)
    recv_gather[me] = send_gather[...]

    pair_copy(P_CARRY, pair_carry, pair_carry_in).wait_recv()
    carry_all[:, other_rows, :] = pair_carry_in[...].astype(f32)

    lines = []
    for k in range(PAGES_DEV):
        rows = slice(k * PAGE, (k + 1) * PAGE)
        rise = jnp.exp2(ccol[rows, :])
        cont = goes_on(dev_page + k)
        w = before[k]
        squares = jnp.zeros((PAGE, DH), f32)
        for h in range(HEADS):
            part = slice(h * 8, h * 8 + 8)
            state = states[k, :, part, :] * cont + carry_all[:, part, :] * w[h : h + 1, :][None]
            qd = (q_ref[rows, head_cols(h)].astype(f32) * rise[:, h : h + 1]).astype(bf16)
            value = mixed[rows, head_cols(h)] + mm(qd, state.reshape(DH, DH).astype(bf16), NT)
            mixed[rows, head_cols(h)] = value
            squares = squares + value * value
        lines.append(mm(jnp.ones((8, DH), f32), squares, NT, highest))

    seq_wait(S_GATHER, src_gather, recv_gather)
    seq_sent(S_GATHER, src_gather, recv_gather)
    decode_squares = jnp.zeros((16, DH), f32)
    for s in range(SEQ):
        soft_ref[s] = recv_gather[s, 0:8, :]
        decode_squares = decode_squares + recv_gather[s, 8:24, :]
    for k in range(PAGES_DEV):
        for n in range(PAGE // DH):
            send_gather[2 * k + n : 2 * k + n + 1, :] = lines[k][0:1, head_cols(n)]
    send_gather[8:24, :] = decode_squares

    def tp_start(hop, _):
        tp_copy(hop).start()
        return 0

    lax.fori_loop(1, TP, tp_start, 0)
    recv_tp[tp] = send_gather[...]

    def tp_wait(hop, _):
        source = lax.rem(tp + TP - hop, TP)
        pltpu.make_async_remote_copy(
            src_ref=send_gather, dst_ref=recv_tp.at[source],
            send_sem=tp_send.at[hop], recv_sem=tp_recv.at[hop],
            device_id=(me, source, rep), device_id_type=MESH,
        ).wait_recv()
        return 0

    lax.fori_loop(1, TP, tp_wait, 0)

    features = TP * HEADS * DH
    gain = gain_ref[...]
    total_squares = recv_tp[0, 8:24, :]
    for t in range(1, TP):
        total_squares = total_squares + recv_tp[t, 8:24, :]
    factor = lax.rsqrt(total_squares / features + norm_eps)[:, 0:8]
    gain_cols = mm(gain, pick, NN, highest)
    for h in range(HEADS):
        dec_ref[h] = dec_own[h] * factor * gain_cols[h : h + 1, :]
    ones = jnp.ones((TP, DH), f32)
    for b in range(ROWS // DH):
        total = mm(recv_tp[:, b, :], ones, TN, highest)
        factor = lax.rsqrt(total / features + norm_eps)
        rows = slice(b * DH, (b + 1) * DH)
        for h in range(HEADS):
            out_ref[rows, head_cols(h)] = (
                mixed[rows, head_cols(h)] * factor * gain[h : h + 1, :]
            ).astype(bf16)

    for which, src, dst in (
        (P_KEYS, ck_ref, other_k),
        (P_VALUES, cv_ref, other_v),
        (P_STATE, pair_state, pair_state_in),
        (P_WEIGHT, pair_weight, pair_weight_in),
        (P_SLOTS, pair_other, pair_slots_in),
        (P_CARRY, pair_carry, pair_carry_in),
        (P_FINAL, pair_final, pair_final_in),
    ):
        pair_copy(which, src, dst).wait_send()
    seq_sent(S_STATE, src_state, recv_state)
    seq_sent(S_SLOTS, src_slots, recv_slots)
    seq_sent(S_SOFT, src_soft, recv_soft)
    seq_sent(S_BACK, src_back, recv_back)

    def tp_sent(hop, _):
        tp_copy(hop).wait_send()
        return 0

    lax.fori_loop(1, TP, tp_sent, 0)


def per_device(
    light_query, light_key, light_value, log_decay, prompt_pages, norm_gain, cache_keys,
    cache_values, step_query, step_key, step_value, step_decay, soft_query, soft_key, soft_value,
):
    vm = pl.BlockSpec(memory_space=pltpu.VMEM)
    V = pltpu.VMEM
    D = pltpu.SemaphoreType.DMA
    out, dec, soft = pl.pallas_call(
        kernel,
        out_shape=(
            jax.ShapeDtypeStruct((ROWS, HEADS * DH), bf16),
            jax.ShapeDtypeStruct((HEADS, 16, 8), f32),
            jax.ShapeDtypeStruct((SEQ, 8, DH), f32),
        ),
        in_specs=[pl.BlockSpec(memory_space=pltpu.SMEM)] + [vm] * 14,
        out_specs=(vm, vm, vm),
        scratch_shapes=[
            V((ROWS, HEADS * DH), f32),
            V((ROWS, HEADS), f32),
            V((PAGES_DEV, HEADS, PAGE), f32),
            V((PAGES_DEV + 1, SEQ, 2 * HALF, DH), f32),
            V((PAGES_DEV, HEADS, DH), f32),
            V((PAGES_DEV, HEADS, DH), f32),
            V((16, HEADS * DH), f32),
            V((16, HEADS * DH), f32),
            V((16, HEADS * DH), f32),
            V((16, HEADS), f32),
            V((DH, DH), f32),
            V((DOCS, STEPS, DH), f32),
            V((DOCS, STEPS, DH), f32),
            V((ROWS, DH), bf16),
            V((ROWS, DH), bf16),
            V((SEQ, HALF, DH), bf16),
            V((SEQ, HALF, DH), bf16),
            V((24, DH), f32),
            V((24, DH), f32),
            V((4, SEQ, HALF, DH), bf16),
            V((2, SEQ, HALF, DH), bf16),
            V((SEQ, HALF + 16, DH), bf16),
            V((SEQ, HALF + 16, DH), bf16),
            V((SEQ, 2, HALF, DH), bf16),
            V((SEQ, 2, HALF, DH), bf16),
            V((SEQ, 16, DH), f32),
            V((SEQ, 16, DH), f32),
            V((SEQ + 1, HALF, DH), f32),
            V((SEQ, HALF, DH), bf16),
            V((SEQ, HALF, DH), bf16),
            V((SEQ, HALF, DH), bf16),
            V((SEQ, HALF, DH), bf16),
            V((SEQ, 2 * HALF, DH), f32),
            V((DOCS, HALF, DH), bf16),
            V((DOCS, HALF, DH), bf16),
            V((DOCS, 2 * HALF, DH), f32),
            V((HEADS, 16, 8), f32),
            V((24, DH), f32),
            V((SEQ, 24, DH), f32),
            V((TP, 24, DH), f32),
            D((7,)),
            D((7,)),
            D((5, SEQ)),
            D((5, SEQ)),
            D((TP,)),
            D((TP,)),
        ],
        compiler_params=pltpu.CompilerParams(
            collective_id=0, has_side_effects=True, vmem_limit_bytes=48 * 1024 * 1024
        ),
        name="attention_block",
    )(
        prompt_pages, light_query, light_key, light_value, log_decay,
        norm_gain.reshape(HEADS, DH), cache_keys, cache_values,
        step_query, step_key, step_value, step_decay, soft_query, soft_key, soft_value,
    )
    light_decode = dec.reshape(HEADS, DOCS, STEPS, 8).transpose(1, 2, 0, 3).astype(bf16)[None]
    soft_decode = soft.reshape(1, DOCS, STEPS, HEADS * DH).astype(bf16)
    return out, light_decode, soft_decode


def solution(mesh):
    prompt = P(("seq", "rep"), "tp")
    sample = P("rep", None, None, "tp")
    return jax.shard_map(
        per_device,
        mesh=mesh,
        in_specs=(prompt,) * 4 + (P(), P("tp")) + (prompt,) * 2 + (sample,) * 7,
        out_specs=(prompt, P("rep", None, None, "tp", "seq"), sample),
        check_vma=False,
    )
```

time: 745 us -> 57.6 us (0.08)
  the two profiles are of different devices: /device:TPU:0 before, /device:TPU:8 now
where the time goes in v1:
time: 57.6 us; the launch traced here: 57 us
  Pallas kernels  42.8 us (74%)
  local copies, waits for them, and re-layouts  13.5 us (23%)
  between operations  0.68 us (1%)
    pallas_call x1, Pallas kernels, per_device(): pl.pallas_call(kernel, out_shape=(jax.ShapeDtypeStruct((ROWS, HEADS * DH)...  42.8 us
    unnamed x26, local copies, waits for them, and re-layouts  12.2 us

profile of v1, /device:TPU:8, one launch (start us, length us, event | category | flops | bytes accessed | tf_op | source)
XLA Modules:
  0.0 57.0 jit_solution(12786409343138234228)
XLA Ops:
  0.6 1.0 %copy.18.g_ref = f32[1024,8]{1,0:T(8,128)S(1)} copy(f32[1024,8]{0,1:T(8,128)} %param.18) | data formatting | bytes 65536 | tf_op args[3]
  1.6 0.0 copy-start
  1.6 1.6 %copy-done = bf16[1024,1024]{1,0:T(8,128)(2,1)S(1)} copy-done((bf16[1024,1024]{1,0:T(8,128)(2,1)S(1)}, bf16[1024,1024]{1,0:T(8,128)(2,1)}, u32[]{:S(2)}) %copy-start) | copy-done | bytes 2097176
  3.2 0.0 copy-start.1
  3.2 0.9 %copy-done.1 = bf16[1024,128]{1,0:T(8,128)(2,1)S(1)} copy-done((bf16[1024,128]{1,0:T(8,128)(2,1)S(1)}, bf16[1024,128]{1,0:T(8,128)(2,1)}, u32[]{:S(2)}) %copy-start.1) | copy-done | bytes 262168
  4.1 0.0 copy-start.2
  4.1 0.9 %copy-done.2 = bf16[1024,128]{1,0:T(8,128)(2,1)S(1)} copy-done((bf16[1024,128]{1,0:T(8,128)(2,1)S(1)}, bf16[1024,128]{1,0:T(8,128)(2,1)}, u32[]{:S(2)}) %copy-start.2) | copy-done | bytes 262168
  5.1 0.0 copy-start.3
  5.1 0.8 %copy-done.3 = bf16[1,4,4,1024]{3,2,1,0:T(4,128)(2,1)S(1)} copy-done((bf16[1,4,4,1024]{3,2,1,0:T(4,128)(2,1)S(1)}, bf16[1,4,4,1024]{3,2,1,0:T(4,128)(2,1)}, u32[]{:S(2)}) %copy-start.3) | copy-done | bytes 32792
  5.8 0.0 copy-start.4
  5.8 0.8 %copy-done.4 = bf16[1,4,4,1024]{3,2,1,0:T(4,128)(2,1)S(1)} copy-done((bf16[1,4,4,1024]{3,2,1,0:T(4,128)(2,1)S(1)}, bf16[1,4,4,1024]{3,2,1,0:T(4,128)(2,1)}, u32[]{:S(2)}) %copy-start.4) | copy-done | bytes 32792
  6.6 0.0 copy-start.5
  6.6 0.8 %copy-done.5 = bf16[1,4,4,1024]{3,2,1,0:T(4,128)(2,1)S(1)} copy-done((bf16[1,4,4,1024]{3,2,1,0:T(4,128)(2,1)S(1)}, bf16[1,4,4,1024]{3,2,1,0:T(4,128)(2,1)}, u32[]{:S(2)}) %copy-start.5) | copy-done | bytes 32792
  7.4 0.0 copy-start.6
  7.4 0.8 %copy-done.6 = bf16[1,4,4,1024]{3,2,1,0:T(4,128)(2,1)S(1)} copy-done((bf16[1,4,4,1024]{3,2,1,0:T(4,128)(2,1)S(1)}, bf16[1,4,4,1024]{3,2,1,0:T(4,128)(2,1)}, u32[]{:S(2)}) %copy-start.6) | copy-done | bytes 32792
  8.1 0.0 copy-start.7
  8.1 0.7 %copy-done.7 = f32[1,4,4,8]{3,2,1,0:T(4,128)S(1)} copy-done((f32[1,4,4,8]{3,2,1,0:T(4,128)S(1)}, f32[1,4,4,8]{3,2,1,0:T(4,128)}, u32[]{:S(2)}) %copy-start.7) | copy-done | bytes 536
  8.8 0.0 copy-start.8
  8.8 0.7 %copy-done.8 = f32[1024]{0:T(1024)S(1)} copy-done((f32[1024]{0:T(1024)S(1)}, f32[1024]{0:T(1024)}, u32[]{:S(2)}) %copy-start.8) | copy-done | bytes 4120
  9.5 0.0 copy-start.9
  9.5 0.7 %copy-done.9 = bf16[1,4,4,128]{3,2,1,0:T(4,128)(2,1)S(1)} copy-done((bf16[1,4,4,128]{3,2,1,0:T(4,128)(2,1)S(1)}, bf16[1,4,4,128]{3,2,1,0:T(4,128)(2,1)}, u32[]{:S(2)}) %copy-start.9) | copy-done | bytes 4120
  10.2 0.0 copy-start.10
  10.2 0.7 %copy-done.10 = bf16[1,4,4,128]{3,2,1,0:T(4,128)(2,1)S(1)} copy-done((bf16[1,4,4,128]{3,2,1,0:T(4,128)(2,1)S(1)}, bf16[1,4,4,128]{3,2,1,0:T(4,128)(2,1)}, u32[]{:S(2)}) %copy-start.10) | copy-done | bytes 4120
  10.9 0.0 copy-start.11
  10.9 0.7 %copy-done.11 = s32[4]{0:T(128)S(1)} copy-done((s32[4]{0:T(128)S(1)}, s32[4]{0:T(128)}, u32[]{:S(2)}) %copy-start.11) | copy-done | bytes 40
  11.5 42.8 %attention_block.1 = (bf16[1024,1024]{1,0:T(8,128)(2,1)S(1)}, f32[8,16,8]{2,1,0:T(8,128)S(1)}, f32[16,8,128]{2,1,0:T(8,128)S(1)}) custom-call(s32[4]{0:T(128)S(1)} %copy-done.11, bf16[1024,1024]{1,0:T(8,128)(2,1)S(1)} %copy-done, bf16[1024,1024]{1,0:T(8,128)(2,1)} %k_ref.1, bf16[1024,1024]{1,0:T(8,128)(2,1)} %v_ref.1, f32[1024,8]{1,0:T(8,128)S(1)} %copy.18.g_ref, ...), custom_call_target="tpu_custom_call" | custom-call | tf_op jit(solution)/shard_map/attention_block/pallas_call | solution.py:511
  54.4 0.6 %copy.21 = bf16[8,4,4,8]{3,0,2,1:T(8,128)(2,1)} copy(bf16[8,4,4,8]{3,2,1,0:T(4,128)(2,1)S(1)} %bitcast.8) | data formatting | bytes 4096 | tf_op jit(solution)/shard_map/convert_element_type | solution.py:577
  55.0 0.6 %convert_element_type.27 = bf16[1,4,4,1024]{3,2,1,0:T(4,128)(2,1)} reshape(bf16[16,8,128]{2,1,0:T(8,128)(2,1)S(1)} %convert_element_type.26) | data formatting | bytes 65536 | tf_op jit(solution)/shard_map/convert_element_type | solution.py:578
  55.7 1.3 %copy.23 = bf16[1024,1024]{1,0:T(8,128)(2,1)} copy(bf16[1024,1024]{1,0:T(8,128)(2,1)S(1)} %get-tuple-element.12) | data formatting | bytes 4194304
  (2 shorter events, 0.0 us)
Async XLA Ops:
  1.6 1.6 %copy-start = (bf16[1024,1024]{1,0:T(8,128)(2,1)S(1)}, bf16[1024,1024]{1,0:T(8,128)(2,1)}, u32[]{:S(2)}) copy-start(bf16[1024,1024]{1,0:T(8,128)(2,1)} %q_ref.1) | copy-start | bytes 6291460
  3.2 0.9 %copy-start.1 = (bf16[1024,128]{1,0:T(8,128)(2,1)S(1)}, bf16[1024,128]{1,0:T(8,128)(2,1)}, u32[]{:S(2)}) copy-start(bf16[1024,128]{1,0:T(8,128)(2,1)} %ck_ref.1) | copy-start | bytes 786436
  4.1 0.9 %copy-start.2 = (bf16[1024,128]{1,0:T(8,128)(2,1)S(1)}, bf16[1024,128]{1,0:T(8,128)(2,1)}, u32[]{:S(2)}) copy-start(bf16[1024,128]{1,0:T(8,128)(2,1)} %cv_ref.1) | copy-start | bytes 786436
  5.1 0.8 %copy-start.3 = (bf16[1,4,4,1024]{3,2,1,0:T(4,128)(2,1)S(1)}, bf16[1,4,4,1024]{3,2,1,0:T(4,128)(2,1)}, u32[]{:S(2)}) copy-start(bf16[1,4,4,1024]{3,2,1,0:T(4,128)(2,1)} %stq_ref.1) | copy-start | bytes 98308
  5.8 0.8 %copy-start.4 = (bf16[1,4,4,1024]{3,2,1,0:T(4,128)(2,1)S(1)}, bf16[1,4,4,1024]{3,2,1,0:T(4,128)(2,1)}, u32[]{:S(2)}) copy-start(bf16[1,4,4,1024]{3,2,1,0:T(4,128)(2,1)} %stk_ref.1) | copy-start | bytes 98308
  6.6 0.8 %copy-start.5 = (bf16[1,4,4,1024]{3,2,1,0:T(4,128)(2,1)S(1)}, bf16[1,4,4,1024]{3,2,1,0:T(4,128)(2,1)}, u32[]{:S(2)}) copy-start(bf16[1,4,4,1024]{3,2,1,0:T(4,128)(2,1)} %stv_ref.1) | copy-start | bytes 98308
  7.4 0.8 %copy-start.6 = (bf16[1,4,4,1024]{3,2,1,0:T(4,128)(2,1)S(1)}, bf16[1,4,4,1024]{3,2,1,0:T(4,128)(2,1)}, u32[]{:S(2)}) copy-start(bf16[1,4,4,1024]{3,2,1,0:T(4,128)(2,1)} %sfq_ref.1) | copy-start | bytes 98308
  8.1 0.7 %copy-start.7 = (f32[1,4,4,8]{3,2,1,0:T(4,128)S(1)}, f32[1,4,4,8]{3,2,1,0:T(4,128)}, u32[]{:S(2)}) copy-start(f32[1,4,4,8]{3,2,1,0:T(4,128)} %std_ref.1) | copy-start | bytes 1540
  8.8 0.7 %copy-start.8 = (f32[1024]{0:T(1024)S(1)}, f32[1024]{0:T(1024)}, u32[]{:S(2)}) copy-start(f32[1024]{0:T(1024)} %param.20) | copy-start | bytes 12292
  9.5 0.7 %copy-start.9 = (bf16[1,4,4,128]{3,2,1,0:T(4,128)(2,1)S(1)}, bf16[1,4,4,128]{3,2,1,0:T(4,128)(2,1)}, u32[]{:S(2)}) copy-start(bf16[1,4,4,128]{3,2,1,0:T(4,128)(2,1)} %sfk_ref.1) | copy-start | bytes 12292
  10.2 0.7 %copy-start.10 = (bf16[1,4,4,128]{3,2,1,0:T(4,128)(2,1)S(1)}, bf16[1,4,4,128]{3,2,1,0:T(4,128)(2,1)}, u32[]{:S(2)}) copy-start(bf16[1,4,4,128]{3,2,1,0:T(4,128)(2,1)} %sfv_ref.1) | copy-start | bytes 12292
  10.9 0.7 %copy-start.11 = (s32[4]{0:T(128)S(1)}, s32[4]{0:T(128)}, u32[]{:S(2)}) copy-start(s32[4]{0:T(128)} %pages_ref.1) | copy-start | bytes 52

commit v2 on v1

--- a/solution.py
+++ b/solution.py
@@ -49,16 +49,18 @@
 
 
 def kernel(
+    pages_in, q_in, k_in, v_in, g_in, gain_in, ck_in, cv_in,
+    stq_in, stk_in, stv_in, std_in, sfq_in, sfk_in, sfv_in,
+    out_ref, dec_ref, soft_ref,
     pages_ref, q_ref, k_ref, v_ref, g_ref, gain_ref, ck_ref, cv_ref,
     stq_ref, stk_ref, stv_ref, std_ref, sfq_ref, sfk_ref, sfv_ref,
-    out_ref, dec_ref, soft_ref,
     mixed, ccol, crow, states, before, weights, stq, stk, stv, std, sfq, sfk, sfv,
     other_k, other_v,
     pair_state, pair_state_in, pair_weight, pair_weight_in, pair_slots, pair_slots_in,
     send_state, recv_state, send_slots, recv_slots, send_soft, recv_soft,
     carry, send_back, recv_back, pair_carry, pair_carry_in, carry_all,
     pair_final, pair_final_in, final_all, dec_own, send_gather, recv_gather, recv_tp,
-    pair_send, pair_recv, seq_send, seq_recv, tp_send, tp_recv,
+    pair_send, pair_recv, seq_send, seq_recv, tp_send, tp_recv, in_sem,
 ):
     me = lax.axis_index("seq")
     tp = lax.axis_index("tp")
@@ -66,6 +68,31 @@
     first_core = rep == 0
     own_rows = pl.ds(pl.multiple_of(rep * HALF, HALF), HALF)
     other_rows = pl.ds(pl.multiple_of((1 - rep) * HALF, HALF), HALF)
+
+    def page_rows(k):
+        return pl.ds(k * PAGE, PAGE)
+
+    inputs = {}
+
+    def fetch(name, src, dst):
+        inputs[name] = pltpu.make_async_copy(src, dst, in_sem.at[len(inputs)])
+        inputs[name].start()
+
+    fetch("pages", pages_in, pages_ref)
+    fetch("g", g_in, g_ref)
+    for k in range(PAGES_DEV):
+        fetch(("k", k), k_in.at[page_rows(k)], k_ref.at[page_rows(k)])
+        fetch(("v", k), v_in.at[page_rows(k)], v_ref.at[page_rows(k)])
+    fetch("q", q_in, q_ref)
+    fetch("ck", ck_in, ck_ref)
+    fetch("cv", cv_in, cv_ref)
+    small = (
+        (stq_in, stq_ref), (stk_in, stk_ref), (stv_in, stv_ref), (std_in, std_ref),
+        (sfq_in, sfq_ref), (sfk_in, sfk_ref), (sfv_in, sfv_ref),
+    )
+    for n, (src, dst) in enumerate(small):
+        fetch(("small", n), src.at[0], dst)
+    fetch("gain", gain_in, gain_ref)
 
     def pair_copy(which, src, dst):
         return pltpu.make_async_remote_copy(
@@ -138,6 +165,7 @@
     lax.fori_loop(1, TP, greet_tp, 0)
     pl.semaphore_signal(barrier, inc=1, device_id=(me, tp, 1 - rep), device_id_type=MESH)
 
+    inputs["pages"].wait()
     ends = []
     for p in range(DOCS):
         ends.append(pages_ref[p] + (ends[-1] if ends else 0))
@@ -172,15 +200,17 @@
     cols_i = lax.broadcasted_iota(jnp.int32, (PAGE, PAGE), 1)
     states[0] = jnp.zeros((SEQ, 2 * HALF, DH), f32)
 
+    inputs["g"].wait()
+
     def state_page(k, carried):
         rows = pl.ds(pl.multiple_of(k * PAGE, PAGE), PAGE)
-        g = g_ref[rows, :] * LOG2E
+        g = g_ref[:, rows] * LOG2E
         lower = (rows_i >= cols_i).astype(f32)
         upper = (rows_i <= cols_i).astype(f32)
-        c = mm(lower, g, NN, highest)
+        c = mm(lower, g, NT, highest)
         ccol[rows, :] = c
-        crow[k] = mm(g, upper, TN, highest)
-        decay = jnp.exp2(mm(g, jnp.ones((PAGE, DH), f32), TN, highest))
+        crow[k] = mm(g, upper, NN, highest)
+        decay = jnp.exp2(mm(g, jnp.ones((PAGE, DH), f32), NN, highest))
         cont = goes_on(dev_page + k)
         before[k] = carried * cont
         keep = decay * cont
@@ -196,7 +226,11 @@
             )
         return after
 
-    total = lax.fori_loop(0, PAGES_DEV, state_page, jnp.ones((HEADS, DH), f32))
+    total = jnp.ones((HEADS, DH), f32)
+    for k in range(PAGES_DEV):
+        inputs[("k", k)].wait()
+        inputs[("v", k)].wait()
+        total = state_page(k, total)
 
     pl.semaphore_wait(barrier, SEQ - 1 + TP - 1 + 1)
     pair_state[...] = states[PAGES_DEV, :, other_rows, :].astype(bf16)
@@ -214,8 +248,8 @@
         pair_slots[2 + s] = (states[slot_page[s] + 1][:, HALF:, :] * slot_valid[s]).astype(bf16)
     pair_other = pair_slots.at[pl.ds((1 - rep) * 2, 2)]
     pair_copy(P_SLOTS, pair_other, pair_slots_in).start()
-    pair_copy(P_KEYS, ck_ref, other_k).start()
-    pair_copy(P_VALUES, cv_ref, other_v).start()
+    pair_copy(P_KEYS, ck_in, other_k).start()
+    pair_copy(P_VALUES, cv_in, other_v).start()
 
     causal = rows_i >= cols_i
 
@@ -236,6 +270,7 @@
 
         lax.fori_loop(first, last, one, 0)
 
+    inputs["q"].wait()
     inside_loop(0, 1)
 
     def half(x):
@@ -270,20 +305,24 @@
     seq_start(S_SLOTS, src_slots, recv_slots)
     recv_slots[me] = send_slots[me]
 
+    for n in range(len(small)):
+        inputs[("small", n)].wait()
+    inputs["ck"].wait()
+    inputs["cv"].wait()
     for p in range(DOCS):
         part = slice(4 * p, 4 * p + 4)
-        stq[part, :] = stq_ref[0, p].astype(f32)
-        stk[part, :] = stk_ref[0, p].astype(f32)
-        stv[part, :] = stv_ref[0, p].astype(f32)
-        std[part, :] = std_ref[0, p]
-        sfk[p] = sfk_ref[0, p].astype(f32)
-        sfv[p] = sfv_ref[0, p].astype(f32)
+        stq[part, :] = stq_ref[p].astype(f32)
+        stk[part, :] = stk_ref[p].astype(f32)
+        stv[part, :] = stv_ref[p].astype(f32)
+        std[part, :] = std_ref[p]
+        sfk[p] = sfk_ref[p].astype(f32)
+        sfv[p] = sfv_ref[p].astype(f32)
         for h in range(HEADS):
-            sfq[pl.ds(p * 32 + h, 4, stride=8), :] = sfq_ref[0, p, :, head_cols(h)].astype(f32)
+            sfq[pl.ds(p * 32 + h, 4, stride=8), :] = sfq_ref[p, :, head_cols(h)].astype(f32)
 
     scale = DH**-0.5 * LOG2E
-    pair_copy(P_KEYS, ck_ref, other_k).wait_recv()
-    pair_copy(P_VALUES, cv_ref, other_v).wait_recv()
+    pair_copy(P_KEYS, ck_in, other_k).wait_recv()
+    pair_copy(P_VALUES, cv_in, other_v).wait_recv()
     queries = sfq[...].astype(bf16)
     query_doc = lax.broadcasted_iota(jnp.int32, (DH, ROWS), 0) // 32
     key_page = lax.broadcasted_iota(jnp.int32, (1, ROWS), 1) // PAGE
@@ -461,6 +500,7 @@
     lax.fori_loop(1, TP, tp_wait, 0)
 
     features = TP * HEADS * DH
+    inputs["gain"].wait()
     gain = gain_ref[...]
     total_squares = recv_tp[0, 8:24, :]
     for t in range(1, TP):
@@ -480,8 +520,8 @@
             ).astype(bf16)
 
     for which, src, dst in (
-        (P_KEYS, ck_ref, other_k),
-        (P_VALUES, cv_ref, other_v),
+        (P_KEYS, ck_in, other_k),
+        (P_VALUES, cv_in, other_v),
         (P_STATE, pair_state, pair_state_in),
         (P_WEIGHT, pair_weight, pair_weight_in),
         (P_SLOTS, pair_other, pair_slots_in),
@@ -515,9 +555,24 @@
             jax.ShapeDtypeStruct((HEADS, 16, 8), f32),
             jax.ShapeDtypeStruct((SEQ, 8, DH), f32),
         ),
-        in_specs=[pl.BlockSpec(memory_space=pltpu.SMEM)] + [vm] * 14,
+        in_specs=[pl.BlockSpec(memory_space=pltpu.HBM)] * 15,
         out_specs=(vm, vm, vm),
         scratch_shapes=[
+            pltpu.SMEM((DOCS,), jnp.int32),
+            V((ROWS, HEADS * DH), bf16),
+            V((ROWS, HEADS * DH), bf16),
+            V((ROWS, HEADS * DH), bf16),
+            V((HEADS, ROWS), f32),
+            V((HEADS, DH), f32),
+            V((ROWS, DH), bf16),
+            V((ROWS, DH), bf16),
+            V((DOCS, STEPS, HEADS * DH), bf16),
+            V((DOCS, STEPS, HEADS * DH), bf16),
+            V((DOCS, STEPS, HEADS * DH), bf16),
+            V((DOCS, STEPS, HEADS), f32),
+            V((DOCS, STEPS, HEADS * DH), bf16),
+            V((DOCS, STEPS, DH), bf16),
+            V((DOCS, STEPS, DH), bf16),
             V((ROWS, HEADS * DH), f32),
             V((ROWS, HEADS), f32),
             V((PAGES_DEV, HEADS, PAGE), f32),
@@ -564,16 +619,17 @@
             D((5, SEQ)),
             D((TP,)),
             D((TP,)),
+            D((21,)),
         ],
         compiler_params=pltpu.CompilerParams(
             collective_id=0, has_side_effects=True, vmem_limit_bytes=48 * 1024 * 1024
         ),
         name="attention_block",
-    )(
-        prompt_pages, light_query, light_key, light_value, log_decay,
+    )(*[pltpu.with_memory_space_constraint(x, pltpu.HBM) for x in (
+        prompt_pages, light_query, light_key, light_value, log_decay.T,
         norm_gain.reshape(HEADS, DH), cache_keys, cache_values,
         step_query, step_key, step_value, step_decay, soft_query, soft_key, soft_value,
-    )
+    )])
     light_decode = dec.reshape(HEADS, DOCS, STEPS, 8).transpose(1, 2, 0, 3).astype(bf16)[None]
     soft_decode = soft.reshape(1, DOCS, STEPS, HEADS * DH).astype(bf16)
     return out, light_decode, soft_decode

time: 57.6 us -> 44.9 us (0.78); the launches traced: 57 us -> 44.9 us
  local copies, waits for them, and re-layouts: 13.5 us -> 2.57 us
  Pallas kernels: 42.8 us -> 41.6 us
    unnamed x26 -> x1, local copies, waits for them, and re-layouts: 12.2 us -> 1.32 us
    pallas_call x1, Pallas kernels: 42.8 us -> 41.6 us  [per_device(): pl.pallas_call(kernel, out_shape=(jax.ShapeDtypeStruct((ROWS, HEADS * DH)...]
where the time goes in v2:
time: 44.9 us
  Pallas kernels  41.6 us (93%)
  local copies, waits for them, and re-layouts  2.57 us (6%)
  between operations  0.65 us (1%)
    pallas_call x1, Pallas kernels, per_device(): pl.pallas_call(kernel, out_shape=(jax.ShapeDtypeStruct((ROWS, HEADS * DH)...  41.6 us
    unnamed x1, local copies, waits for them, and re-layouts  1.32 us

profile of v2, /device:TPU:8, one launch (start us, length us, event | category | flops | bytes accessed | tf_op | source)
XLA Modules:
  0.0 44.9 jit_solution(9181790855160747462)
XLA Ops:
  0.6 41.6 %attention_block.1 = (bf16[1024,1024]{1,0:T(8,128)(2,1)S(1)}, f32[8,16,8]{2,1,0:T(8,128)S(1)}, f32[16,8,128]{2,1,0:T(8,128)S(1)}) custom-call(s32[4]{0:T(128)} %pages_in.1, bf16[1024,1024]{1,0:T(8,128)(2,1)} %q_in.1, bf16[1024,1024]{1,0:T(8,128)(2,1)} %k_in.1, bf16[1024,1024]{1,0:T(8,128)(2,1)} %v_in.1, f32[8,1024]{1,0:T(8,128)} %bitcast.9, ...), custom_call_target="tpu_custom_call" | custom-call | tf_op jit(solution)/shard_map/attention_block/pallas_call | solution.py:551
  42.3 0.6 %copy.20 = bf16[8,4,4,8]{3,0,2,1:T(8,128)(2,1)} copy(bf16[8,4,4,8]{3,2,1,0:T(4,128)(2,1)S(1)} %bitcast.8) | data formatting | bytes 4096 | tf_op jit(solution)/shard_map/convert_element_type | solution.py:633
  42.9 0.6 %convert_element_type.27 = bf16[1,4,4,1024]{3,2,1,0:T(4,128)(2,1)} reshape(bf16[16,8,128]{2,1,0:T(8,128)(2,1)S(1)} %convert_element_type.26) | data formatting | bytes 65536 | tf_op jit(solution)/shard_map/convert_element_type | solution.py:634
  43.5 1.3 %copy.22 = bf16[1024,1024]{1,0:T(8,128)(2,1)} copy(bf16[1024,1024]{1,0:T(8,128)(2,1)S(1)} %get-tuple-element.12) | data formatting | bytes 4194304
  (2 shorter events, 0.0 us)

commit v3 on v2

--- a/solution.py
+++ b/solution.py
@@ -31,7 +31,7 @@
 TN = (((0,), (0,)), ((), ()))
 
 P_KEYS, P_VALUES, P_STATE, P_WEIGHT, P_SLOTS, P_CARRY, P_FINAL = range(7)
-S_STATE, S_SLOTS, S_SOFT, S_BACK, S_GATHER = range(5)
+S_STATE, S_SLOTS, S_SOFT, S_BACK, S_RESULT, S_DECODE = range(6)
 
 
 def mm(a, b, dims, precision=None):
@@ -51,15 +51,15 @@
 def kernel(
     pages_in, q_in, k_in, v_in, g_in, gain_in, ck_in, cv_in,
     stq_in, stk_in, stv_in, std_in, sfq_in, sfk_in, sfv_in,
-    out_ref, dec_ref, soft_ref,
-    pages_ref, q_ref, k_ref, v_ref, g_ref, gain_ref, ck_ref, cv_ref,
+    mixed, sums_ref, dec_own, soft_ref, gain_ref,
+    pages_ref, q_ref, k_ref, v_ref, g_ref, ck_ref, cv_ref,
     stq_ref, stk_ref, stv_ref, std_ref, sfq_ref, sfk_ref, sfv_ref,
-    mixed, ccol, crow, states, before, weights, stq, stk, stv, std, sfq, sfk, sfv,
+    ccol, crow, states, before, weights, stq, stk, stv, std, sfq, sfk, sfv,
     other_k, other_v,
     pair_state, pair_state_in, pair_weight, pair_weight_in, pair_slots, pair_slots_in,
     send_state, recv_state, send_slots, recv_slots, send_soft, recv_soft,
     carry, send_back, recv_back, pair_carry, pair_carry_in, carry_all,
-    pair_final, pair_final_in, final_all, dec_own, send_gather, recv_gather, recv_tp,
+    pair_final, pair_final_in, final_all, send_result, recv_result, send_decode, recv_decode, send_tp,
     pair_send, pair_recv, seq_send, seq_recv, tp_send, tp_recv, in_sem,
 ):
     me = lax.axis_index("seq")
@@ -109,60 +109,46 @@
         )
 
     def seq_start(phase, src, dst):
-        def one(hop, _):
+        for hop in range(1, SEQ):
             seq_copy(phase, src, dst, hop).start()
-            return 0
-
-        lax.fori_loop(1, SEQ, one, 0)
 
     def seq_wait(phase, src, dst):
-        def one(hop, _):
+        for hop in range(1, SEQ):
             source = lax.rem(me + SEQ - hop, SEQ)
             pltpu.make_async_remote_copy(
                 src_ref=src(source), dst_ref=dst.at[source],
                 send_sem=seq_send.at[phase, hop], recv_sem=seq_recv.at[phase, hop],
                 device_id=(source, tp, rep), device_id_type=MESH,
             ).wait_recv()
-            return 0
-
-        lax.fori_loop(1, SEQ, one, 0)
 
     def seq_sent(phase, src, dst):
-        def one(hop, _):
+        for hop in range(1, SEQ):
             seq_copy(phase, src, dst, hop).wait_send()
-            return 0
-
-        lax.fori_loop(1, SEQ, one, 0)
 
     src_state = lambda t: send_state.at[t]
     src_slots = lambda t: send_slots.at[t]
     src_soft = lambda t: send_soft.at[t]
     src_back = lambda t: send_back.at[t]
-    src_gather = lambda t: send_gather
+    src_result = lambda t: send_result
+    src_decode = lambda t: send_decode
 
     def tp_copy(hop):
         return pltpu.make_async_remote_copy(
-            src_ref=send_gather, dst_ref=recv_tp.at[tp],
+            src_ref=send_tp, dst_ref=sums_ref.at[tp],
             send_sem=tp_send.at[hop], recv_sem=tp_recv.at[hop],
             device_id=(me, lax.rem(tp + hop, TP), rep), device_id_type=MESH,
         )
 
     barrier = pltpu.get_barrier_semaphore()
 
-    def greet_seq(hop, _):
+    for hop in range(1, SEQ):
         pl.semaphore_signal(
             barrier, inc=1, device_id=(lax.rem(me + hop, SEQ), tp, rep), device_id_type=MESH
         )
-        return 0
-
-    def greet_tp(hop, _):
+    for hop in range(1, TP):
         pl.semaphore_signal(
             barrier, inc=1, device_id=(me, lax.rem(tp + hop, TP), rep), device_id_type=MESH
         )
-        return 0
-
-    lax.fori_loop(1, SEQ, greet_seq, 0)
-    lax.fori_loop(1, TP, greet_tp, 0)
     pl.semaphore_signal(barrier, inc=1, device_id=(me, tp, 1 - rep), device_id_type=MESH)
 
     inputs["pages"].wait()
@@ -201,16 +187,29 @@
     states[0] = jnp.zeros((SEQ, 2 * HALF, DH), f32)
 
     inputs["g"].wait()
+    g = g_ref[...] * LOG2E
+    g_high = g.astype(bf16)
+    g_rest = g - g_high.astype(f32)
+    g_mid = g_rest.astype(bf16)
+    g_low = (g_rest - g_mid.astype(f32)).astype(bf16)
+    upper = (rows_i <= cols_i).astype(f32).astype(bf16)
+    parts = [
+        x[:, k * PAGE : (k + 1) * PAGE].astype(f32)
+        for x in (g_high, g_mid, g_low)
+        for k in range(PAGES_DEV)
+    ]
+    summed = mm(jnp.concatenate(parts, axis=0).astype(bf16), upper, NN)
+    wide = PAGES_DEV * HEADS
+    summed = summed[0:wide] + summed[wide : 2 * wide] + summed[2 * wide :]
+    turned = jnp.transpose(summed)
 
     def state_page(k, carried):
-        rows = pl.ds(pl.multiple_of(k * PAGE, PAGE), PAGE)
-        g = g_ref[:, rows] * LOG2E
-        lower = (rows_i >= cols_i).astype(f32)
-        upper = (rows_i <= cols_i).astype(f32)
-        c = mm(lower, g, NT, highest)
+        rows = page_rows(k)
+        c = turned[:, k * HEADS : (k + 1) * HEADS]
         ccol[rows, :] = c
-        crow[k] = mm(g, upper, NN, highest)
-        decay = jnp.exp2(mm(g, jnp.ones((PAGE, DH), f32), NN, highest))
+        line = summed[k * HEADS : (k + 1) * HEADS]
+        crow[k] = line
+        decay = jnp.exp2(jnp.broadcast_to(line[:, PAGE - 1 : PAGE], (HEADS, DH)))
         cont = goes_on(dev_page + k)
         before[k] = carried * cont
         keep = decay * cont
@@ -359,8 +358,6 @@
     seq_start(S_BACK, src_back, recv_back)
     recv_back[me] = send_back[me]
 
-    inside_loop(1, 3)
-
     seq_wait(S_SLOTS, src_slots, recv_slots)
     for p in range(DOCS):
         last_page = jnp.clip(ends[p] - 1, 0, 2 * PAGES_DEV * SEQ - 1)
@@ -378,14 +375,70 @@
         pair_final[p] = final.astype(bf16)
     pair_copy(P_FINAL, pair_final, pair_final_in).start()
 
-    inside_loop(3, 4)
-
-    seq_wait(S_BACK, src_back, recv_back)
-    carry0 = recv_back[...].astype(f32)
-    carry1 = expand(w0[0])[None] * carry0 + state0
-    carry_all[:, own_rows, :] = lax.select(first_core, carry0, carry1)
-    pair_carry[...] = lax.select(first_core, carry1, carry0).astype(bf16)
-    pair_copy(P_CARRY, pair_carry, pair_carry_in).start()
+    def iota(shape, dim):
+        return lax.broadcasted_iota(jnp.int32, shape, dim)
+
+    chain = jnp.logical_and(
+        iota((16, 16), 0) // STEPS == iota((16, 16), 1) // STEPS, iota((16, 16), 0) >= iota((16, 16), 1)
+    )
+    fall = mm(chain.astype(f32), std[...] * LOG2E, NN, highest)
+    spread_heads = (iota((HEADS, DH), 1) // 16 == iota((HEADS, DH), 0)).astype(f32)
+    fall_from = mm(fall, spread_heads, NN, highest)
+    lane_step = jnp.bitwise_and(iota((16, DH), 1), 15)
+    diagonal = jnp.where(lane_step == iota((16, DH), 0), fall_from, 0.0)
+    fall_to = mm(jnp.ones((16, 16), f32), diagonal, NN, highest)
+    linked = jnp.logical_and(
+        iota((16, DH), 0) // STEPS == lane_step // STEPS, iota((16, DH), 0) >= lane_step
+    )
+    met = jnp.concatenate(
+        [
+            mm(stq[:, head_cols(h)].astype(bf16), stk[:, head_cols(h)].astype(bf16), NT)
+            for h in range(HEADS)
+        ],
+        axis=1,
+    )
+    met = jnp.where(linked, met * jnp.exp2(fall_from - fall_to), 0.0)
+    cols = HEADS * 8
+    pick = (iota((DH, cols), 0) == jnp.bitwise_and(iota((DH, cols), 1), 7) + me * 8).astype(f32)
+    values = jnp.concatenate([stv[:, head_cols(h)] for h in range(HEADS)], axis=0)
+    values = mm(values.astype(bf16), pick.astype(bf16), NN)
+    values = jnp.where(iota((DH, cols), 0) // 16 == iota((DH, cols), 1) // 8, values, 0.0)
+    decoded = mm(met, values, NN, highest)
+    spread_cols = (iota((HEADS, cols), 1) // 8 == iota((HEADS, cols), 0)).astype(f32)
+    shrunk = jnp.exp2(mm(fall, spread_cols, NN, highest))
+    wide = HEADS * HALF
+    fold = jnp.logical_and(
+        iota((wide, cols), 0) // HALF == iota((wide, cols), 1) // 8,
+        jnp.bitwise_and(iota((wide, cols), 0), 7) == jnp.bitwise_and(iota((wide, cols), 1), 7),
+    ).astype(f32).astype(bf16)
+    same = jnp.bitwise_and(iota((16, wide), 1), HALF - 1) // 8 == iota((16, wide), 0) // STEPS
+
+    inside_loop(1, 2)
+
+    pair_copy(P_FINAL, pair_final, pair_final_in).wait_recv()
+    final_all[:, other_rows, :] = pair_final_in[...].astype(f32)
+    read = jnp.concatenate(
+        [
+            mm(
+                stq[:, head_cols(h)].astype(bf16),
+                final_all[:, h * 8 : h * 8 + 8, :].reshape(DOCS * 8, DH).astype(bf16),
+                NT,
+            )
+            for h in range(HEADS)
+        ],
+        axis=1,
+    )
+    read = jnp.where(same, read, 0.0)
+    read_high = read.astype(bf16)
+    read_low = (read - read_high.astype(f32)).astype(bf16)
+    read = mm(read_high, fold, NN) + mm(read_low, fold, NN)
+    decoded = decoded + read * shrunk
+    dec_own[...] = decoded
+    squares = mm(jnp.ones((8, cols), f32), decoded * decoded, NT, highest)
+    send_decode[...] = jnp.zeros((1, DH), f32)
+    send_decode[:, 0:16] = squares[0:1, :]
+    seq_start(S_DECODE, src_decode, recv_decode)
+    recv_decode[me] = send_decode[...]
 
     seq_wait(S_SOFT, src_soft, recv_soft)
     doc = me // STEPS
@@ -414,42 +467,20 @@
         e = lax.select(step >= i, jnp.exp2(own[i] - top), jnp.zeros((8, 1), f32))
         numer = numer + e.astype(bf16).astype(f32) * own_v[i : i + 1, :]
         amount = amount + e
-    send_gather[0:8, :] = numer / amount
-
-    pair_copy(P_FINAL, pair_final, pair_final_in).wait_recv()
-    final_all[:, other_rows, :] = pair_final_in[...].astype(f32)
-    t16 = lax.broadcasted_iota(jnp.int32, (16, 16), 0)
-    s16 = lax.broadcasted_iota(jnp.int32, (16, 16), 1)
-    chain = jnp.logical_and(t16 // STEPS == s16 // STEPS, t16 >= s16)
-    chain_t = jnp.logical_and(t16 // STEPS == s16 // STEPS, t16 <= s16)
-    fall = std[...] * LOG2E
-    fall_col = mm(chain.astype(f32), fall, NN, highest)
-    fall_row = mm(fall, chain_t.astype(f32), TN, highest)
-    f128 = lax.broadcasted_iota(jnp.int32, (DH, 8), 0)
-    c128 = lax.broadcasted_iota(jnp.int32, (DH, 8), 1)
-    pick = (f128 == c128 + me * 8).astype(f32)
-    r32 = lax.broadcasted_iota(jnp.int32, (32, 8), 0)
-    c32 = lax.broadcasted_iota(jnp.int32, (32, 8), 1)
-    fold = (jnp.bitwise_and(r32, 7) == c32).astype(f32)
-    t32 = lax.broadcasted_iota(jnp.int32, (16, 32), 0)
-    p32 = lax.broadcasted_iota(jnp.int32, (16, 32), 1)
-    same = t32 // STEPS == p32 // 8
-    squares = jnp.zeros((16, 8), f32)
-    for h in range(HEADS):
-        q = stq[:, head_cols(h)]
-        k = stk[:, head_cols(h)]
-        v = mm(stv[:, head_cols(h)], pick, NN, highest)
-        spread = jnp.exp2(fall_col[:, h : h + 1] - fall_row[h : h + 1, :])
-        grid = jnp.where(chain, mm(q, k, NT, highest) * spread, 0.0)
-        final = final_all[:, h * 8 : h * 8 + 8, :].reshape(32, DH)
-        read = jnp.where(same, mm(q, final, NT, highest), 0.0)
-        value = mm(read, fold, NN, highest) * jnp.exp2(fall_col[:, h : h + 1])
-        value = value + mm(grid, v, NN, highest)
-        dec_own[h] = value
-        squares = squares + value * value
-    send_gather[8:24, :] = mm(squares, jnp.ones((8, DH), f32), NN, highest)
-    seq_start(S_GATHER, src_gather, recv_gather)
-    recv_gather[me] = send_gather[...]
+    send_result[...] = numer / amount
+    seq_start(S_RESULT, src_result, recv_result)
+    recv_result[me] = send_result[...]
+
+    inside_loop(2, 3)
+
+    seq_wait(S_BACK, src_back, recv_back)
+    carry0 = recv_back[...].astype(f32)
+    carry1 = expand(w0[0])[None] * carry0 + state0
+    carry_all[:, own_rows, :] = lax.select(first_core, carry0, carry1)
+    pair_carry[...] = lax.select(first_core, carry1, carry0).astype(bf16)
+    pair_copy(P_CARRY, pair_carry, pair_carry_in).start()
+
+    inside_loop(3, 4)
 
     pair_copy(P_CARRY, pair_carry, pair_carry_in).wait_recv()
     carry_all[:, other_rows, :] = pair_carry_in[...].astype(f32)
@@ -470,54 +501,28 @@
             squares = squares + value * value
         lines.append(mm(jnp.ones((8, DH), f32), squares, NT, highest))
 
-    seq_wait(S_GATHER, src_gather, recv_gather)
-    seq_sent(S_GATHER, src_gather, recv_gather)
-    decode_squares = jnp.zeros((16, DH), f32)
-    for s in range(SEQ):
-        soft_ref[s] = recv_gather[s, 0:8, :]
-        decode_squares = decode_squares + recv_gather[s, 8:24, :]
+    seq_wait(S_RESULT, src_result, recv_result)
+    soft_ref[...] = recv_result[...]
+    seq_wait(S_DECODE, src_decode, recv_decode)
+    decode_squares = recv_decode[0]
+    for s in range(1, SEQ):
+        decode_squares = decode_squares + recv_decode[s]
     for k in range(PAGES_DEV):
         for n in range(PAGE // DH):
-            send_gather[2 * k + n : 2 * k + n + 1, :] = lines[k][0:1, head_cols(n)]
-    send_gather[8:24, :] = decode_squares
-
-    def tp_start(hop, _):
+            send_tp[2 * k + n : 2 * k + n + 1, :] = lines[k][0:1, head_cols(n)]
+    send_tp[8:16, :] = jnp.broadcast_to(decode_squares, (8, DH))
+
+    for hop in range(1, TP):
         tp_copy(hop).start()
-        return 0
-
-    lax.fori_loop(1, TP, tp_start, 0)
-    recv_tp[tp] = send_gather[...]
-
-    def tp_wait(hop, _):
+    sums_ref[tp] = send_tp[...]
+    inputs["gain"].wait()
+    for hop in range(1, TP):
         source = lax.rem(tp + TP - hop, TP)
         pltpu.make_async_remote_copy(
-            src_ref=send_gather, dst_ref=recv_tp.at[source],
+            src_ref=send_tp, dst_ref=sums_ref.at[source],
             send_sem=tp_send.at[hop], recv_sem=tp_recv.at[hop],
             device_id=(me, source, rep), device_id_type=MESH,
         ).wait_recv()
-        return 0
-
-    lax.fori_loop(1, TP, tp_wait, 0)
-
-    features = TP * HEADS * DH
-    inputs["gain"].wait()
-    gain = gain_ref[...]
-    total_squares = recv_tp[0, 8:24, :]
-    for t in range(1, TP):
-        total_squares = total_squares + recv_tp[t, 8:24, :]
-    factor = lax.rsqrt(total_squares / features + norm_eps)[:, 0:8]
-    gain_cols = mm(gain, pick, NN, highest)
-    for h in range(HEADS):
-        dec_ref[h] = dec_own[h] * factor * gain_cols[h : h + 1, :]
-    ones = jnp.ones((TP, DH), f32)
-    for b in range(ROWS // DH):
-        total = mm(recv_tp[:, b, :], ones, TN, highest)
-        factor = lax.rsqrt(total / features + norm_eps)
-        rows = slice(b * DH, (b + 1) * DH)
-        for h in range(HEADS):
-            out_ref[rows, head_cols(h)] = (
-                mixed[rows, head_cols(h)] * factor * gain[h : h + 1, :]
-            ).astype(bf16)
 
     for which, src, dst in (
         (P_KEYS, ck_in, other_k),
@@ -534,11 +539,56 @@
     seq_sent(S_SOFT, src_soft, recv_soft)
     seq_sent(S_BACK, src_back, recv_back)
 
-    def tp_sent(hop, _):
+    seq_sent(S_RESULT, src_result, recv_result)
+    seq_sent(S_DECODE, src_decode, recv_decode)
+    for hop in range(1, TP):
         tp_copy(hop).wait_send()
-        return 0
-
-    lax.fori_loop(1, TP, tp_sent, 0)
+
+
+def norm_kernel(
+    mixed, sums, decoded, soft, gain_ref, out_hbm, dec_hbm, soft_hbm, block, dec_lines, dec_block, soft_block, sem
+):
+    me = lax.axis_index("seq")
+    features = TP * HEADS * DH
+    copies = []
+
+    def send(src, dst):
+        copy = pltpu.make_async_copy(src, dst, sem.at[len(copies)])
+        copy.start()
+        copies.append(copy)
+
+    gain = gain_ref[...]
+    ones = jnp.ones((TP, DH), f32)
+    for b in range(ROWS // DH):
+        total = mm(sums[:, b, :], ones, TN, highest)
+        factor = lax.rsqrt(total / features + norm_eps)
+        rows = slice(b * DH, (b + 1) * DH)
+        for h in range(HEADS):
+            block[rows, head_cols(h)] = (
+                mixed[rows, head_cols(h)] * factor * gain[h : h + 1, :]
+            ).astype(bf16)
+        send(block.at[rows], out_hbm.at[rows])
+
+    def iota(shape, dim):
+        return lax.broadcasted_iota(jnp.int32, shape, dim)
+
+    cols = HEADS * 8
+    pick = (iota((DH, cols), 0) == jnp.bitwise_and(iota((DH, cols), 1), 7) + me * 8).astype(f32)
+    gain_cols = mm(gain, pick, NN, highest)
+    gain_cols = jnp.where(iota((HEADS, cols), 1) // 8 == iota((HEADS, cols), 0), gain_cols, 0.0)
+    gain_cols = jnp.sum(gain_cols, axis=0, keepdims=True)
+    total = mm(sums[:, 8, :], jnp.ones((TP, cols), f32), TN, highest)[0:16]
+    value = decoded[...] * lax.rsqrt(total / features + norm_eps) * gain_cols
+    for h in range(HEADS):
+        dec_lines[pl.ds(h, 16, stride=8), :] = value[:, h * 8 : h * 8 + 8]
+    dec_block[...] = dec_lines[...].reshape(DOCS, STEPS, HEADS, 8).astype(bf16)
+    send(dec_block, dec_hbm.at[0])
+    for p in range(DOCS):
+        for h in range(HEADS):
+            soft_block[p, :, head_cols(h)] = soft[pl.ds(p * 32 + h, 4, stride=8), :].astype(bf16)
+    send(soft_block, soft_hbm.at[0])
+    for copy in copies:
+        copy.wait()
 
 
 def per_device(
@@ -548,22 +598,23 @@
     vm = pl.BlockSpec(memory_space=pltpu.VMEM)
     V = pltpu.VMEM
     D = pltpu.SemaphoreType.DMA
-    out, dec, soft = pl.pallas_call(
+    mixed, sums, dec, soft, gain = pl.pallas_call(
         kernel,
         out_shape=(
-            jax.ShapeDtypeStruct((ROWS, HEADS * DH), bf16),
-            jax.ShapeDtypeStruct((HEADS, 16, 8), f32),
+            jax.ShapeDtypeStruct((ROWS, HEADS * DH), f32),
+            jax.ShapeDtypeStruct((TP, 16, DH), f32),
+            jax.ShapeDtypeStruct((16, HEADS * 8), f32),
             jax.ShapeDtypeStruct((SEQ, 8, DH), f32),
+            jax.ShapeDtypeStruct((HEADS, DH), f32),
         ),
         in_specs=[pl.BlockSpec(memory_space=pltpu.HBM)] * 15,
-        out_specs=(vm, vm, vm),
+        out_specs=(vm,) * 5,
         scratch_shapes=[
             pltpu.SMEM((DOCS,), jnp.int32),
             V((ROWS, HEADS * DH), bf16),
             V((ROWS, HEADS * DH), bf16),
             V((ROWS, HEADS * DH), bf16),
             V((HEADS, ROWS), f32),
-            V((HEADS, DH), f32),
             V((ROWS, DH), bf16),
             V((ROWS, DH), bf16),
             V((DOCS, STEPS, HEADS * DH), bf16),
@@ -573,7 +624,6 @@
             V((DOCS, STEPS, HEADS * DH), bf16),
             V((DOCS, STEPS, DH), bf16),
             V((DOCS, STEPS, DH), bf16),
-            V((ROWS, HEADS * DH), f32),
             V((ROWS, HEADS), f32),
             V((PAGES_DEV, HEADS, PAGE), f32),
             V((PAGES_DEV + 1, SEQ, 2 * HALF, DH), f32),
@@ -609,14 +659,15 @@
             V((DOCS, HALF, DH), bf16),
             V((DOCS, HALF, DH), bf16),
             V((DOCS, 2 * HALF, DH), f32),
-            V((HEADS, 16, 8), f32),
-            V((24, DH), f32),
-            V((SEQ, 24, DH), f32),
-            V((TP, 24, DH), f32),
+            V((8, DH), f32),
+            V((SEQ, 8, DH), f32),
+            V((1, DH), f32),
+            V((SEQ, 1, DH), f32),
+            V((16, DH), f32),
             D((7,)),
             D((7,)),
-            D((5, SEQ)),
-            D((5, SEQ)),
+            D((6, SEQ)),
+            D((6, SEQ)),
             D((TP,)),
             D((TP,)),
             D((21,)),
@@ -630,9 +681,26 @@
         norm_gain.reshape(HEADS, DH), cache_keys, cache_values,
         step_query, step_key, step_value, step_decay, soft_query, soft_key, soft_value,
     )])
-    light_decode = dec.reshape(HEADS, DOCS, STEPS, 8).transpose(1, 2, 0, 3).astype(bf16)[None]
-    soft_decode = soft.reshape(1, DOCS, STEPS, HEADS * DH).astype(bf16)
-    return out, light_decode, soft_decode
+    hbm = pl.BlockSpec(memory_space=pl.ANY)
+    return pl.pallas_call(
+        norm_kernel,
+        out_shape=(
+            jax.ShapeDtypeStruct((ROWS, HEADS * DH), bf16),
+            jax.ShapeDtypeStruct((1, DOCS, STEPS, HEADS, 8), bf16),
+            jax.ShapeDtypeStruct((1, DOCS, STEPS, HEADS * DH), bf16),
+        ),
+        in_specs=[vm] * 5,
+        out_specs=(hbm,) * 3,
+        scratch_shapes=[
+            V((ROWS, HEADS * DH), bf16),
+            V((16 * HEADS, 8), f32),
+            V((DOCS, STEPS, HEADS, 8), bf16),
+            V((DOCS, STEPS, HEADS * DH), bf16),
+            D((10,)),
+        ],
+        compiler_params=pltpu.CompilerParams(vmem_limit_bytes=16 * 1024 * 1024),
+        name="norms",
+    )(mixed, sums, dec, soft.reshape(SEQ * 8, DH), gain)
 
 
 def solution(mesh):

time: 44.9 us -> 37.8 us (0.84)
  the two profiles are of different devices: /device:TPU:8 before, /device:TPU:1 now
where the time goes in v3:
time: 37.8 us; the launch traced here: 37.7 us
  Pallas kernels  37.1 us (98%)
  between operations  0.64 us (2%)
    pallas_call x1, Pallas kernels, per_device(): pl.pallas_call(kernel, out_shape=(jax.ShapeDtypeStruct((ROWS, HEADS * DH)...  35.3 us
    pallas_call x1, Pallas kernels, per_device(): pl.pallas_call(norm_kernel, out_shape=(jax.ShapeDtypeStruct((ROWS, HEADS...  1.8 us

profile of v3, /device:TPU:1, one launch (start us, length us, event | category | flops | bytes accessed | tf_op | source)
XLA Modules:
  0.0 37.7 jit_solution(19002983552562031)
XLA Ops:
  0.6 35.3 %attention_block.1 = (f32[1024,1024]{1,0:T(8,128)S(1)}, f32[8,16,128]{2,1,0:T(8,128)S(1)}, f32[16,64]{1,0:T(8,128)S(1)}, f32[16,8,128]{2,1,0:T(8,128)S(1)}, f32[8,128]{1,0:T(8,128)S(1)}) custom-call(s32[4]{0:T(128)} %pages_in.1, bf16[1024,1024]{1,0:T(8,128)(2,1)} %q_in.1, bf16[1024,1024]{1,0:T(8,128)(2,1)} %k_in.1, bf16[1024,1024]{1,0:T(8,128)(2,1)} %v_in.1, ...), custom_call_target="tpu_custom_call" | custom-call | tf_op jit(solution)/shard_map/attention_block/pallas_call | solution.py:601
  35.9 1.8 %norms.1 = (bf16[1024,1024]{1,0:T(8,128)(2,1)}, bf16[1,4,4,8,8]{4,3,2,1,0:T(8,128)(2,1)}, bf16[1,4,4,1024]{3,2,1,0:T(4,128)(2,1)}) custom-call(f32[1024,1024]{1,0:T(8,128)S(1)} %get-tuple-element.8.mixed, f32[8,16,128]{2,1,0:T(8,128)S(1)} %get-tuple-element.9.sums, f32[16,64]{1,0:T(8,128)S(1)} %get-tuple-element.10.decoded, f32[128,128]{1,0:T(8,128)S(1)} %bitcast.3, ...), custom_call_target="tpu_custom_call" | custom-call | tf_op jit(solution)/shard_map/norms/pallas_call | solution.py:685

commit v4 on v3

--- a/solution.py
+++ b/solution.py
@@ -30,7 +30,9 @@
 NT = (((1,), (1,)), ((), ()))
 TN = (((0,), (0,)), ((), ()))
 
-P_KEYS, P_VALUES, P_STATE, P_WEIGHT, P_SLOTS, P_CARRY, P_FINAL = range(7)
+P_KEYS, P_VALUES, P_STATE, P_WEIGHT, P_SLOTS, P_CARRY, P_FINAL, P_QUERY = range(8)
+SEQ_HOPS = (10, 6, 9, 11, 14, 2, 8, 5, 7, 13, 15, 1, 3, 4, 12)
+TP_HOPS = (4, 3, 5, 2, 6, 1, 7)
 S_STATE, S_SLOTS, S_SOFT, S_BACK, S_RESULT, S_DECODE = range(6)
 
 
@@ -55,11 +57,11 @@
     pages_ref, q_ref, k_ref, v_ref, g_ref, ck_ref, cv_ref,
     stq_ref, stk_ref, stv_ref, std_ref, sfq_ref, sfk_ref, sfv_ref,
     ccol, crow, states, before, weights, stq, stk, stv, std, sfq, sfk, sfv,
-    other_k, other_v,
+    other_k, other_v, other_q, query_all, read_rows,
     pair_state, pair_state_in, pair_weight, pair_weight_in, pair_slots, pair_slots_in,
     send_state, recv_state, send_slots, recv_slots, send_soft, recv_soft,
     carry, send_back, recv_back, pair_carry, pair_carry_in, carry_all,
-    pair_final, pair_final_in, final_all, send_result, recv_result, send_decode, recv_decode, send_tp,
+    pair_final, pair_final_in, final_all, square_sums, send_result, recv_result, send_decode, recv_decode, send_tp,
     pair_send, pair_recv, seq_send, seq_recv, tp_send, tp_recv, in_sem,
 ):
     me = lax.axis_index("seq")
@@ -94,6 +96,14 @@
         fetch(("small", n), src.at[0], dst)
     fetch("gain", gain_in, gain_ref)
 
+    me_x, me_y = me // 4, lax.rem(me, 4)
+
+    def seq_ahead(hop):
+        return lax.rem(me_x + hop // 4, 4) * 4 + lax.rem(me_y + hop % 4, 4)
+
+    def seq_behind(hop):
+        return lax.rem(me_x + 4 - hop // 4, 4) * 4 + lax.rem(me_y + 4 - hop % 4, 4)
+
     def pair_copy(which, src, dst):
         return pltpu.make_async_remote_copy(
             src_ref=src, dst_ref=dst, send_sem=pair_send.at[which], recv_sem=pair_recv.at[which],
@@ -101,7 +111,7 @@
         )
 
     def seq_copy(phase, src, dst, hop):
-        target = lax.rem(me + hop, SEQ)
+        target = seq_ahead(hop)
         return pltpu.make_async_remote_copy(
             src_ref=src(target), dst_ref=dst.at[me],
             send_sem=seq_send.at[phase, hop], recv_sem=seq_recv.at[phase, hop],
@@ -109,12 +119,12 @@
         )
 
     def seq_start(phase, src, dst):
-        for hop in range(1, SEQ):
+        for hop in SEQ_HOPS:
             seq_copy(phase, src, dst, hop).start()
 
     def seq_wait(phase, src, dst):
-        for hop in range(1, SEQ):
-            source = lax.rem(me + SEQ - hop, SEQ)
+        for hop in SEQ_HOPS:
+            source = seq_behind(hop)
             pltpu.make_async_remote_copy(
                 src_ref=src(source), dst_ref=dst.at[source],
                 send_sem=seq_send.at[phase, hop], recv_sem=seq_recv.at[phase, hop],
@@ -122,7 +132,7 @@
             ).wait_recv()
 
     def seq_sent(phase, src, dst):
-        for hop in range(1, SEQ):
+        for hop in SEQ_HOPS:
             seq_copy(phase, src, dst, hop).wait_send()
 
     src_state = lambda t: send_state.at[t]
@@ -141,11 +151,11 @@
 
     barrier = pltpu.get_barrier_semaphore()
 
-    for hop in range(1, SEQ):
+    for hop in SEQ_HOPS:
         pl.semaphore_signal(
-            barrier, inc=1, device_id=(lax.rem(me + hop, SEQ), tp, rep), device_id_type=MESH
+            barrier, inc=1, device_id=(seq_ahead(hop), tp, rep), device_id_type=MESH
         )
-    for hop in range(1, TP):
+    for hop in TP_HOPS:
         pl.semaphore_signal(
             barrier, inc=1, device_id=(me, lax.rem(tp + hop, TP), rep), device_id_type=MESH
         )
@@ -168,17 +178,19 @@
     def doc_of(page):
         return sum((e <= page).astype(jnp.int32) for e in ends)
 
-    slot_page, slot_valid = [], []
+    slot_page, slot_valid, slot_doc = [], [], []
     inside = [flag(jnp.logical_and(e > chip_page, e < chip_page + 2 * PAGES_DEV)) for e in ends]
     for s in range(2):
-        place = 0
+        place, owner = 0, 0
         for p in range(DOCS):
             rank = sum(inside[:p]) if p else 0
             place = place + inside[p] * flag(rank == s) * (ends[p] - chip_page)
+            owner = owner + inside[p] * flag(rank == s) * p
         local = place - 1 - rep * PAGES_DEV
         ok = jnp.logical_and(
             place > 0, jnp.logical_and(local >= 0, local < PAGES_DEV)
         )
+        slot_doc.append(owner)
         slot_page.append(jnp.clip(local, 0, PAGES_DEV - 1))
         slot_valid.append(jnp.where(ok, 1.0, 0.0).astype(f32))
 
@@ -231,7 +243,6 @@
         inputs[("v", k)].wait()
         total = state_page(k, total)
 
-    pl.semaphore_wait(barrier, SEQ - 1 + TP - 1 + 1)
     pair_state[...] = states[PAGES_DEV, :, other_rows, :].astype(bf16)
     pair_weight[0:8] = total
     for s in range(2):
@@ -240,6 +251,7 @@
             pick = jnp.where(slot_page[s] == k, slot_valid[s], 0.0).astype(f32)
             w = w + pick * weights[k]
         pair_weight[8 + 8 * s : 16 + 8 * s] = w
+    pl.semaphore_wait(barrier, SEQ - 1 + TP - 1 + 1)
     pair_copy(P_STATE, pair_state, pair_state_in).start()
     pair_copy(P_WEIGHT, pair_weight, pair_weight_in).start()
     for s in range(2):
@@ -247,6 +259,7 @@
         pair_slots[2 + s] = (states[slot_page[s] + 1][:, HALF:, :] * slot_valid[s]).astype(bf16)
     pair_other = pair_slots.at[pl.ds((1 - rep) * 2, 2)]
     pair_copy(P_SLOTS, pair_other, pair_slots_in).start()
+    pair_copy(P_QUERY, stq_in.at[0], other_q).start()
     pair_copy(P_KEYS, ck_in, other_k).start()
     pair_copy(P_VALUES, cv_in, other_v).start()
 
@@ -269,8 +282,6 @@
 
         lax.fori_loop(first, last, one, 0)
 
-    inputs["q"].wait()
-    inside_loop(0, 1)
 
     def half(x):
         return lax.select(first_core, x[0:4], x[4:8])
@@ -294,20 +305,8 @@
     seq_start(S_STATE, src_state, recv_state)
     recv_state[me] = send_state[me]
 
-    pair_copy(P_SLOTS, pair_other, pair_slots_in).wait_recv()
-    for s in range(2):
-        own_slot = states[slot_page[s] + 1][:, 0:HALF, :]
-        own_slot = lax.select(first_core, own_slot, states[slot_page[s] + 1][:, HALF:, :])
-        slot = own_slot * slot_valid[s] + pair_slots_in[s].astype(f32)
-        slot = slot + expand(w1[1 + s])[None] * state0
-        send_slots[:, s] = slot.astype(bf16)
-    seq_start(S_SLOTS, src_slots, recv_slots)
-    recv_slots[me] = send_slots[me]
-
     for n in range(len(small)):
         inputs[("small", n)].wait()
-    inputs["ck"].wait()
-    inputs["cv"].wait()
     for p in range(DOCS):
         part = slice(4 * p, 4 * p + 4)
         stq[part, :] = stq_ref[p].astype(f32)
@@ -319,64 +318,35 @@
         for h in range(HEADS):
             sfq[pl.ds(p * 32 + h, 4, stride=8), :] = sfq_ref[p, :, head_cols(h)].astype(f32)
 
-    scale = DH**-0.5 * LOG2E
-    pair_copy(P_KEYS, ck_in, other_k).wait_recv()
-    pair_copy(P_VALUES, cv_in, other_v).wait_recv()
-    queries = sfq[...].astype(bf16)
-    query_doc = lax.broadcasted_iota(jnp.int32, (DH, ROWS), 0) // 32
-    key_page = lax.broadcasted_iota(jnp.int32, (1, ROWS), 1) // PAGE
-    score, here = [], []
-    for base, key_block in ((dev_page, ck_ref), (chip_page + (1 - rep) * PAGES_DEV, other_k)):
-        score.append(mm(queries, key_block[...], NT) * scale)
-        here.append(query_doc == jnp.broadcast_to(doc_of(key_page + base), (DH, ROWS)))
-    peak = jnp.maximum(
-        *[
-            jnp.max(jnp.where(m, s, mask_low), axis=1, keepdims=True)
-            for m, s in zip(here, score)
-        ]
-    )
-    chance = [jnp.where(m, jnp.exp2(s - peak), 0.0) for m, s in zip(here, score)]
-    amount = sum(jnp.sum(x, axis=1, keepdims=True) for x in chance)
-    numer = mm(chance[0].astype(bf16), cv_ref[...], NN) + mm(
-        chance[1].astype(bf16), other_v[...], NN
-    )
-    lane = lax.broadcasted_iota(jnp.int32, (DH, DH), 1)
-    both = jnp.where(lane < 64, jnp.broadcast_to(peak, (DH, DH)), jnp.broadcast_to(amount, (DH, DH)))
-    send_soft[:, 0:8, :] = numer.reshape(SEQ, 8, DH)
-    send_soft[:, 8:16, :] = both.reshape(SEQ, 8, DH)
-    seq_start(S_SOFT, src_soft, recv_soft)
-    recv_soft[me] = send_soft[me]
-
-    seq_wait(S_STATE, src_state, recv_state)
-    running = jnp.zeros((HALF, DH), f32)
-    for j in range(SEQ):
-        carry[j] = running
-        send_back[j] = running.astype(bf16)
-        rows = recv_state[j, HALF:, :].astype(f32)
-        running = expand(rows[0:4] + rows[8:12]) * running + recv_state[j, 0:HALF, :].astype(f32)
-    carry[SEQ] = running
-    seq_start(S_BACK, src_back, recv_back)
-    recv_back[me] = send_back[me]
-
-    seq_wait(S_SLOTS, src_slots, recv_slots)
-    for p in range(DOCS):
-        last_page = jnp.clip(ends[p] - 1, 0, 2 * PAGES_DEV * SEQ - 1)
-        chip = lax.shift_right_logical(last_page, 3)
-        chip_last = jnp.bitwise_and(last_page, 7) == 7
-        rank = sum(
-            [flag(lax.shift_right_logical(ends[o] - 1, 3) == chip) for o in range(p)],
-            jnp.int32(0),
-        )
-        rows = recv_state[chip][HALF:, :].astype(f32)
-        w = expand(rows[4:8] + rows[12:16]) * jnp.where(rank == 0, 1.0, 0.0).astype(f32)
-        ended = recv_slots[chip, jnp.minimum(rank, 1)].astype(f32) + w * carry[chip]
-        final = lax.select(chip_last, carry[chip + 1], ended)
-        final_all[p, own_rows, :] = final
-        pair_final[p] = final.astype(bf16)
-    pair_copy(P_FINAL, pair_final, pair_final_in).start()
+    pair_copy(P_QUERY, stq_in.at[0], other_q).wait_recv()
+    other_lines = jnp.concatenate([other_q[p].astype(f32) for p in range(DOCS)], axis=0)
+    query_all[pl.ds(pl.multiple_of(rep * 16, 16), 16), :] = stq[...].astype(bf16)
+    query_all[pl.ds(pl.multiple_of((1 - rep) * 16, 16), 16), :] = other_lines.astype(bf16)
+
+    def half_query(n):
+        return query_all[:, pl.ds(pl.multiple_of((rep * (HEADS // 2) + n) * DH, DH), DH)]
 
     def iota(shape, dim):
         return lax.broadcasted_iota(jnp.int32, shape, dim)
+
+    pair_copy(P_SLOTS, pair_other, pair_slots_in).wait_recv()
+    slots = []
+    for s in range(2):
+        own_slot = states[slot_page[s] + 1][:, 0:HALF, :]
+        own_slot = lax.select(first_core, own_slot, states[slot_page[s] + 1][:, HALF:, :])
+        slot = own_slot * slot_valid[s] + pair_slots_in[s].astype(f32)
+        slots.append(slot + expand(w1[1 + s])[None] * state0)
+    lane_doc = jnp.bitwise_and(iota((DH, 32), 1), 15) // STEPS
+    reads = []
+    for n in range(HEADS // 2):
+        read = jnp.zeros((DH, 32), f32)
+        for s in range(2):
+            state = slots[s][:, n * 8 : n * 8 + 8, :].reshape(DH, DH).astype(bf16)
+            read = read + jnp.where(lane_doc == slot_doc[s], mm(state, half_query(n), NT), 0.0)
+        reads.append(read)
+    send_slots[...] = jnp.concatenate(reads, axis=1).reshape(SEQ, 8, DH)
+    seq_start(S_SLOTS, src_slots, recv_slots)
+    recv_slots[me] = send_slots[me]
 
     chain = jnp.logical_and(
         iota((16, 16), 0) // STEPS == iota((16, 16), 1) // STEPS, iota((16, 16), 0) >= iota((16, 16), 1)
@@ -406,32 +376,83 @@
     decoded = mm(met, values, NN, highest)
     spread_cols = (iota((HEADS, cols), 1) // 8 == iota((HEADS, cols), 0)).astype(f32)
     shrunk = jnp.exp2(mm(fall, spread_cols, NN, highest))
-    wide = HEADS * HALF
-    fold = jnp.logical_and(
-        iota((wide, cols), 0) // HALF == iota((wide, cols), 1) // 8,
-        jnp.bitwise_and(iota((wide, cols), 0), 7) == jnp.bitwise_and(iota((wide, cols), 1), 7),
-    ).astype(f32).astype(bf16)
-    same = jnp.bitwise_and(iota((16, wide), 1), HALF - 1) // 8 == iota((16, wide), 0) // STEPS
-
-    inside_loop(1, 2)
+
+    inputs["ck"].wait()
+    inputs["cv"].wait()
+    scale = DH**-0.5 * LOG2E
+    pair_copy(P_KEYS, ck_in, other_k).wait_recv()
+    pair_copy(P_VALUES, cv_in, other_v).wait_recv()
+    queries = sfq[...].astype(bf16)
+    query_doc = lax.broadcasted_iota(jnp.int32, (DH, ROWS), 0) // 32
+    key_page = lax.broadcasted_iota(jnp.int32, (1, ROWS), 1) // PAGE
+    score, here = [], []
+    for base, key_block in ((dev_page, ck_ref), (chip_page + (1 - rep) * PAGES_DEV, other_k)):
+        score.append(mm(queries, key_block[...], NT) * scale)
+        here.append(query_doc == jnp.broadcast_to(doc_of(key_page + base), (DH, ROWS)))
+    peak = jnp.maximum(
+        *[
+            jnp.max(jnp.where(m, s, mask_low), axis=1, keepdims=True)
+            for m, s in zip(here, score)
+        ]
+    )
+    chance = [jnp.where(m, jnp.exp2(s - peak), 0.0) for m, s in zip(here, score)]
+    amount = sum(jnp.sum(x, axis=1, keepdims=True) for x in chance)
+    numer = mm(chance[0].astype(bf16), cv_ref[...], NN) + mm(
+        chance[1].astype(bf16), other_v[...], NN
+    )
+    lane = lax.broadcasted_iota(jnp.int32, (DH, DH), 1)
+    both = jnp.where(lane < 64, jnp.broadcast_to(peak, (DH, DH)), jnp.broadcast_to(amount, (DH, DH)))
+    send_soft[:, 0:8, :] = numer.reshape(SEQ, 8, DH)
+    send_soft[:, 8:16, :] = both.reshape(SEQ, 8, DH)
+    seq_start(S_SOFT, src_soft, recv_soft)
+    recv_soft[me] = send_soft[me]
+
+    seq_wait(S_STATE, src_state, recv_state)
+    running = jnp.zeros((HALF, DH), f32)
+    for j in range(SEQ):
+        carry[j] = running
+        send_back[j] = running.astype(bf16)
+        rows = recv_state[j, HALF:, :].astype(f32)
+        running = expand(rows[0:4] + rows[8:12]) * running + recv_state[j, 0:HALF, :].astype(f32)
+    carry[SEQ] = running
+    seq_start(S_BACK, src_back, recv_back)
+    recv_back[me] = send_back[me]
+
+    seq_wait(S_SLOTS, src_slots, recv_slots)
+    for p in range(DOCS):
+        last_page = jnp.clip(ends[p] - 1, 0, 2 * PAGES_DEV * SEQ - 1)
+        chip = lax.shift_right_logical(last_page, 3)
+        chip_last = jnp.bitwise_and(last_page, 7) == 7
+        rank = sum(
+            [flag(lax.shift_right_logical(ends[o] - 1, 3) == chip) for o in range(p)],
+            jnp.int32(0),
+        )
+        rows = recv_state[chip][HALF:, :].astype(f32)
+        w = expand(rows[4:8] + rows[12:16]) * jnp.where(rank == 0, 1.0, 0.0).astype(f32)
+        final_all[p] = lax.select(chip_last, carry[chip + 1], w * carry[chip])
+    tile = recv_slots[0]
+    for j in range(1, SEQ):
+        tile = tile + recv_slots[j]
+    reads = []
+    for n in range(HEADS // 2):
+        state = final_all[:, n * 8 : n * 8 + 8, :].reshape(DOCS * 8, DH).astype(bf16)
+        read = mm(state, half_query(n), NT)
+        read = jnp.where(iota((32, 32), 0) // 8 == lane_doc[0:32], read, 0.0)
+        reads.append(read[0:8] + read[8:16] + read[16:24] + read[24:32])
+    pair_final[...] = tile + jnp.concatenate(reads, axis=1)
+    pair_copy(P_FINAL, pair_final, pair_final_in).start()
+
+    inputs["q"].wait()
+    inside_loop(0, 1)
 
     pair_copy(P_FINAL, pair_final, pair_final_in).wait_recv()
-    final_all[:, other_rows, :] = pair_final_in[...].astype(f32)
-    read = jnp.concatenate(
-        [
-            mm(
-                stq[:, head_cols(h)].astype(bf16),
-                final_all[:, h * 8 : h * 8 + 8, :].reshape(DOCS * 8, DH).astype(bf16),
-                NT,
-            )
-            for h in range(HEADS)
-        ],
-        axis=1,
-    )
-    read = jnp.where(same, read, 0.0)
-    read_high = read.astype(bf16)
-    read_low = (read - read_high.astype(f32)).astype(bf16)
-    read = mm(read_high, fold, NN) + mm(read_low, fold, NN)
+    own_tile, got_tile = pair_final[...], pair_final_in[...]
+    tiles = [lax.select(first_core, own_tile, got_tile), lax.select(first_core, got_tile, own_tile)]
+    read_rows[...] = jnp.transpose(jnp.concatenate(tiles, axis=0))
+    lines_of = [
+        read_rows[pl.ds(pl.multiple_of(n * 32 + rep * 16, 16), 16), :] for n in range(HEADS // 2)
+    ]
+    read = jnp.concatenate([x[:, 8 * n : 8 * n + 8] for n in range(2) for x in lines_of], axis=1)
     decoded = decoded + read * shrunk
     dec_own[...] = decoded
     squares = mm(jnp.ones((8, cols), f32), decoded * decoded, NT, highest)
@@ -439,6 +460,16 @@
     send_decode[:, 0:16] = squares[0:1, :]
     seq_start(S_DECODE, src_decode, recv_decode)
     recv_decode[me] = send_decode[...]
+
+    inside_loop(1, 4)
+
+    seq_wait(S_BACK, src_back, recv_back)
+    carry0 = recv_back[...].astype(f32)
+    carry1 = expand(w0[0])[None] * carry0 + state0
+    carry_all[:, own_rows, :] = lax.select(first_core, carry0, carry1)
+    pair_carry[...] = lax.select(first_core, carry1, carry0).astype(bf16)
+    pair_copy(P_CARRY, pair_carry, pair_carry_in).start()
+
 
     seq_wait(S_SOFT, src_soft, recv_soft)
     doc = me // STEPS
@@ -471,23 +502,10 @@
     seq_start(S_RESULT, src_result, recv_result)
     recv_result[me] = send_result[...]
 
-    inside_loop(2, 3)
-
-    seq_wait(S_BACK, src_back, recv_back)
-    carry0 = recv_back[...].astype(f32)
-    carry1 = expand(w0[0])[None] * carry0 + state0
-    carry_all[:, own_rows, :] = lax.select(first_core, carry0, carry1)
-    pair_carry[...] = lax.select(first_core, carry1, carry0).astype(bf16)
-    pair_copy(P_CARRY, pair_carry, pair_carry_in).start()
-
-    inside_loop(3, 4)
-
     pair_copy(P_CARRY, pair_carry, pair_carry_in).wait_recv()
     carry_all[:, other_rows, :] = pair_carry_in[...].astype(f32)
-
-    lines = []
     for k in range(PAGES_DEV):
-        rows = slice(k * PAGE, (k + 1) * PAGE)
+        rows = page_rows(k)
         rise = jnp.exp2(ccol[rows, :])
         cont = goes_on(dev_page + k)
         w = before[k]
@@ -499,24 +517,27 @@
             value = mixed[rows, head_cols(h)] + mm(qd, state.reshape(DH, DH).astype(bf16), NT)
             mixed[rows, head_cols(h)] = value
             squares = squares + value * value
-        lines.append(mm(jnp.ones((8, DH), f32), squares, NT, highest))
-
-    seq_wait(S_RESULT, src_result, recv_result)
-    soft_ref[...] = recv_result[...]
+        high = squares.astype(bf16)
+        rest = (squares - high.astype(f32)).astype(bf16)
+        ones = jnp.ones((16, DH), bf16)
+        line = mm(ones, high, NT) + mm(ones, rest, NT)
+        for n in range(PAGE // DH):
+            send_tp[2 * k + n : 2 * k + n + 1, :] = line[0:1, head_cols(n)]
+
+
     seq_wait(S_DECODE, src_decode, recv_decode)
     decode_squares = recv_decode[0]
     for s in range(1, SEQ):
         decode_squares = decode_squares + recv_decode[s]
-    for k in range(PAGES_DEV):
-        for n in range(PAGE // DH):
-            send_tp[2 * k + n : 2 * k + n + 1, :] = lines[k][0:1, head_cols(n)]
     send_tp[8:16, :] = jnp.broadcast_to(decode_squares, (8, DH))
 
-    for hop in range(1, TP):
+    for hop in TP_HOPS:
         tp_copy(hop).start()
     sums_ref[tp] = send_tp[...]
+    seq_wait(S_RESULT, src_result, recv_result)
+    soft_ref[...] = recv_result[...]
     inputs["gain"].wait()
-    for hop in range(1, TP):
+    for hop in TP_HOPS:
         source = lax.rem(tp + TP - hop, TP)
         pltpu.make_async_remote_copy(
             src_ref=send_tp, dst_ref=sums_ref.at[source],
@@ -525,6 +546,7 @@
         ).wait_recv()
 
     for which, src, dst in (
+        (P_QUERY, stq_in.at[0], other_q),
         (P_KEYS, ck_in, other_k),
         (P_VALUES, cv_in, other_v),
         (P_STATE, pair_state, pair_state_in),
@@ -541,7 +563,7 @@
 
     seq_sent(S_RESULT, src_result, recv_result)
     seq_sent(S_DECODE, src_decode, recv_decode)
-    for hop in range(1, TP):
+    for hop in TP_HOPS:
         tp_copy(hop).wait_send()
 
 
@@ -558,11 +580,12 @@
         copies.append(copy)
 
     gain = gain_ref[...]
-    ones = jnp.ones((TP, DH), f32)
+    lines = jnp.concatenate([sums[:, b, :] for b in range(ROWS // DH)], axis=1)
+    total = mm(lines, jnp.ones((TP, DH), f32), TN, highest)
+    factors = lax.rsqrt(total / features + norm_eps)
     for b in range(ROWS // DH):
-        total = mm(sums[:, b, :], ones, TN, highest)
-        factor = lax.rsqrt(total / features + norm_eps)
         rows = slice(b * DH, (b + 1) * DH)
+        factor = factors[rows]
         for h in range(HEADS):
             block[rows, head_cols(h)] = (
                 mixed[rows, head_cols(h)] * factor * gain[h : h + 1, :]
@@ -638,6 +661,9 @@
             V((DOCS, STEPS, DH), f32),
             V((ROWS, DH), bf16),
             V((ROWS, DH), bf16),
+            V((DOCS, STEPS, HEADS * DH), bf16),
+            V((32, HEADS * DH), bf16),
+            V((DH, 16), f32),
             V((SEQ, HALF, DH), bf16),
             V((SEQ, HALF, DH), bf16),
             V((24, DH), f32),
@@ -646,8 +672,8 @@
             V((2, SEQ, HALF, DH), bf16),
             V((SEQ, HALF + 16, DH), bf16),
             V((SEQ, HALF + 16, DH), bf16),
-            V((SEQ, 2, HALF, DH), bf16),
-            V((SEQ, 2, HALF, DH), bf16),
+            V((SEQ, 8, DH), f32),
+            V((SEQ, 8, DH), f32),
             V((SEQ, 16, DH), f32),
             V((SEQ, 16, DH), f32),
             V((SEQ + 1, HALF, DH), f32),
@@ -656,16 +682,17 @@
             V((SEQ, HALF, DH), bf16),
             V((SEQ, HALF, DH), bf16),
             V((SEQ, 2 * HALF, DH), f32),
-            V((DOCS, HALF, DH), bf16),
-            V((DOCS, HALF, DH), bf16),
-            V((DOCS, 2 * HALF, DH), f32),
+            V((8, DH), f32),
+            V((8, DH), f32),
+            V((DOCS, HALF, DH), f32),
+            V((ROWS, DH), f32),
             V((8, DH), f32),
             V((SEQ, 8, DH), f32),
             V((1, DH), f32),
             V((SEQ, 1, DH), f32),
             V((16, DH), f32),
-            D((7,)),
-            D((7,)),
+            D((8,)),
+            D((8,)),
             D((6, SEQ)),
             D((6, SEQ)),
             D((TP,)),

time: 37.8 us -> 36.4 us (0.963)
  Pallas kernels: 37.1 us -> 35.7 us
    pallas_call x1, Pallas kernels: 35.3 us -> 33.6 us  [per_device(): pl.pallas_call(kernel, out_shape=(jax.ShapeDtypeStruct((ROWS, HEADS * DH)...]
where the time goes in v4:
time: 36.4 us
  Pallas kernels  35.7 us (98%)
  between operations  0.64 us (2%)
    pallas_call x1, Pallas kernels, per_device(): pl.pallas_call(kernel, out_shape=(jax.ShapeDtypeStruct((ROWS, HEADS * DH)...  33.6 us
    pallas_call x1, Pallas kernels, per_device(): pl.pallas_call(norm_kernel, out_shape=(jax.ShapeDtypeStruct((ROWS, HEADS...  2.08 us

profile of v4, /device:TPU:1, one launch (start us, length us, event | category | flops | bytes accessed | tf_op | source)
XLA Modules:
  0.0 36.4 jit_solution(15636695202521141176)
XLA Ops:
  0.6 33.6 %attention_block.1 = (f32[1024,1024]{1,0:T(8,128)S(1)}, f32[8,16,128]{2,1,0:T(8,128)S(1)}, f32[16,64]{1,0:T(8,128)S(1)}, f32[16,8,128]{2,1,0:T(8,128)S(1)}, f32[8,128]{1,0:T(8,128)S(1)}) custom-call(s32[4]{0:T(128)} %pages_in.1, bf16[1024,1024]{1,0:T(8,128)(2,1)} %q_in.1, bf16[1024,1024]{1,0:T(8,128)(2,1)} %k_in.1, bf16[1024,1024]{1,0:T(8,128)(2,1)} %v_in.1, ...), custom_call_target="tpu_custom_call" | custom-call | tf_op jit(solution)/shard_map/attention_block/pallas_call | solution.py:624
  34.3 2.1 %norms.1 = (bf16[1024,1024]{1,0:T(8,128)(2,1)}, bf16[1,4,4,8,8]{4,3,2,1,0:T(8,128)(2,1)}, bf16[1,4,4,1024]{3,2,1,0:T(4,128)(2,1)}) custom-call(f32[1024,1024]{1,0:T(8,128)S(1)} %get-tuple-element.8.mixed, f32[8,16,128]{2,1,0:T(8,128)S(1)} %get-tuple-element.9.sums, f32[16,64]{1,0:T(8,128)S(1)} %get-tuple-element.10.decoded, f32[128,128]{1,0:T(8,128)S(1)} %bitcast.3, ...), custom_call_target="tpu_custom_call" | custom-call | tf_op jit(solution)/shard_map/norms/pallas_call | solution.py:712

commit v5 on v4

--- a/solution.py
+++ b/solution.py
@@ -269,11 +269,15 @@
         rows = pl.ds(pl.multiple_of(k * PAGE, PAGE), PAGE)
         c = ccol[rows, :]
         r = crow[k]
+        rise = jnp.exp2(c)
         for h in range(HEADS):
             scores = mm(q_ref[rows, head_cols(h)], k_ref[rows, head_cols(h)], NT)
             grid = jnp.exp2(c[:, h : h + 1] - r[h : h + 1, :])
             block = jnp.where(causal, scores * grid, 0.0).astype(bf16)
             mixed[rows, head_cols(h)] = mm(block, v_ref[rows, head_cols(h)], NN)
+            q_ref[rows, head_cols(h)] = (
+                q_ref[rows, head_cols(h)].astype(f32) * rise[:, h : h + 1]
+            ).astype(bf16)
 
     def inside_loop(first, last):
         def one(k, _):
@@ -506,14 +510,13 @@
     carry_all[:, other_rows, :] = pair_carry_in[...].astype(f32)
     for k in range(PAGES_DEV):
         rows = page_rows(k)
-        rise = jnp.exp2(ccol[rows, :])
         cont = goes_on(dev_page + k)
         w = before[k]
         squares = jnp.zeros((PAGE, DH), f32)
         for h in range(HEADS):
             part = slice(h * 8, h * 8 + 8)
             state = states[k, :, part, :] * cont + carry_all[:, part, :] * w[h : h + 1, :][None]
-            qd = (q_ref[rows, head_cols(h)].astype(f32) * rise[:, h : h + 1]).astype(bf16)
+            qd = q_ref[rows, head_cols(h)]
             value = mixed[rows, head_cols(h)] + mm(qd, state.reshape(DH, DH).astype(bf16), NT)
             mixed[rows, head_cols(h)] = value
             squares = squares + value * value
@@ -580,12 +583,13 @@
         copies.append(copy)
 
     gain = gain_ref[...]
-    lines = jnp.concatenate([sums[:, b, :] for b in range(ROWS // DH)], axis=1)
-    total = mm(lines, jnp.ones((TP, DH), f32), TN, highest)
+    total = sums[0, 0:8, :]
+    for t in range(1, TP):
+        total = total + sums[t, 0:8, :]
     factors = lax.rsqrt(total / features + norm_eps)
     for b in range(ROWS // DH):
         rows = slice(b * DH, (b + 1) * DH)
-        factor = factors[rows]
+        factor = jnp.transpose(jnp.broadcast_to(factors[b : b + 1, :], (DH, DH)))
         for h in range(HEADS):
             block[rows, head_cols(h)] = (
                 mixed[rows, head_cols(h)] * factor * gain[h : h + 1, :]

time: 36.4 us -> 35.6 us (0.978)
  Pallas kernels: 35.7 us -> 34.9 us
    pallas_call x1, Pallas kernels: 2.08 us -> 1.59 us  [per_device(): pl.pallas_call(norm_kernel, out_shape=(jax.ShapeDtypeStruct((ROWS, HEADS...]
where the time goes in v5:
time: 35.6 us
  Pallas kernels  34.9 us (98%)
  between operations  0.64 us (2%)
    pallas_call x1, Pallas kernels, per_device(): pl.pallas_call(kernel, out_shape=(jax.ShapeDtypeStruct((ROWS, HEADS * DH)...  33.3 us
    pallas_call x1, Pallas kernels, per_device(): pl.pallas_call(norm_kernel, out_shape=(jax.ShapeDtypeStruct((ROWS, HEADS...  1.59 us

profile of v5, /device:TPU:1, one launch (start us, length us, event | category | flops | bytes accessed | tf_op | source)
XLA Modules:
  0.0 35.6 jit_solution(14421047143105238797)
XLA Ops:
  0.6 33.3 %attention_block.1 = (f32[1024,1024]{1,0:T(8,128)S(1)}, f32[8,16,128]{2,1,0:T(8,128)S(1)}, f32[16,64]{1,0:T(8,128)S(1)}, f32[16,8,128]{2,1,0:T(8,128)S(1)}, f32[8,128]{1,0:T(8,128)S(1)}) custom-call(s32[4]{0:T(128)} %pages_in.1, bf16[1024,1024]{1,0:T(8,128)(2,1)} %q_in.1, bf16[1024,1024]{1,0:T(8,128)(2,1)} %k_in.1, bf16[1024,1024]{1,0:T(8,128)(2,1)} %v_in.1, ...), custom_call_target="tpu_custom_call" | custom-call | tf_op jit(solution)/shard_map/attention_block/pallas_call | solution.py:628
  34.0 1.6 %norms.1 = (bf16[1024,1024]{1,0:T(8,128)(2,1)}, bf16[1,4,4,8,8]{4,3,2,1,0:T(8,128)(2,1)}, bf16[1,4,4,1024]{3,2,1,0:T(4,128)(2,1)}) custom-call(f32[1024,1024]{1,0:T(8,128)S(1)} %get-tuple-element.8.mixed, f32[8,16,128]{2,1,0:T(8,128)S(1)} %get-tuple-element.9.sums, f32[16,64]{1,0:T(8,128)S(1)} %get-tuple-element.10.decoded, f32[128,128]{1,0:T(8,128)S(1)} %bitcast.3, ...), custom_call_target="tpu_custom_call" | custom-call | tf_op jit(solution)/shard_map/norms/pallas_call | solution.py:716

commit v6 on v5

--- a/solution.py
+++ b/solution.py
@@ -71,6 +71,71 @@
     own_rows = pl.ds(pl.multiple_of(rep * HALF, HALF), HALF)
     other_rows = pl.ds(pl.multiple_of((1 - rep) * HALF, HALF), HALF)
 
+    me_x, me_y = me // 4, lax.rem(me, 4)
+
+    def seq_ahead(hop):
+        return lax.rem(me_x + hop // 4, 4) * 4 + lax.rem(me_y + hop % 4, 4)
+
+    def seq_behind(hop):
+        return lax.rem(me_x + 4 - hop // 4, 4) * 4 + lax.rem(me_y + 4 - hop % 4, 4)
+
+    def pair_copy(which, src, dst):
+        return pltpu.make_async_remote_copy(
+            src_ref=src, dst_ref=dst, send_sem=pair_send.at[which], recv_sem=pair_recv.at[which],
+            device_id=(me, tp, 1 - rep), device_id_type=MESH,
+        )
+
+    def seq_copy(phase, src, dst, hop):
+        target = seq_ahead(hop)
+        return pltpu.make_async_remote_copy(
+            src_ref=src(target), dst_ref=dst.at[me],
+            send_sem=seq_send.at[phase, hop], recv_sem=seq_recv.at[phase, hop],
+            device_id=(target, tp, rep), device_id_type=MESH,
+        )
+
+    def seq_start(phase, src, dst):
+        for hop in SEQ_HOPS:
+            seq_copy(phase, src, dst, hop).start()
+
+    def seq_wait(phase, src, dst):
+        for hop in SEQ_HOPS:
+            source = seq_behind(hop)
+            pltpu.make_async_remote_copy(
+                src_ref=src(source), dst_ref=dst.at[source],
+                send_sem=seq_send.at[phase, hop], recv_sem=seq_recv.at[phase, hop],
+                device_id=(source, tp, rep), device_id_type=MESH,
+            ).wait_recv()
+
+    def seq_sent(phase, src, dst):
+        for hop in SEQ_HOPS:
+            seq_copy(phase, src, dst, hop).wait_send()
+
+    src_state = lambda t: send_state.at[t]
+    src_slots = lambda t: send_slots.at[t]
+    src_soft = lambda t: send_soft.at[t]
+    src_back = lambda t: send_back.at[t]
+    src_result = lambda t: send_result
+    src_decode = lambda t: send_decode
+
+    def tp_copy(hop):
+        return pltpu.make_async_remote_copy(
+            src_ref=send_tp, dst_ref=sums_ref.at[tp],
+            send_sem=tp_send.at[hop], recv_sem=tp_recv.at[hop],
+            device_id=(me, lax.rem(tp + hop, TP), rep), device_id_type=MESH,
+        )
+
+    barrier = pltpu.get_barrier_semaphore()
+
+    for hop in SEQ_HOPS:
+        pl.semaphore_signal(
+            barrier, inc=1, device_id=(seq_ahead(hop), tp, rep), device_id_type=MESH
+        )
+    for hop in TP_HOPS:
+        pl.semaphore_signal(
+            barrier, inc=1, device_id=(me, lax.rem(tp + hop, TP), rep), device_id_type=MESH
+        )
+    pl.semaphore_signal(barrier, inc=1, device_id=(me, tp, 1 - rep), device_id_type=MESH)
+
     def page_rows(k):
         return pl.ds(k * PAGE, PAGE)
 
@@ -95,71 +160,6 @@
     for n, (src, dst) in enumerate(small):
         fetch(("small", n), src.at[0], dst)
     fetch("gain", gain_in, gain_ref)
-
-    me_x, me_y = me // 4, lax.rem(me, 4)
-
-    def seq_ahead(hop):
-        return lax.rem(me_x + hop // 4, 4) * 4 + lax.rem(me_y + hop % 4, 4)
-
-    def seq_behind(hop):
-        return lax.rem(me_x + 4 - hop // 4, 4) * 4 + lax.rem(me_y + 4 - hop % 4, 4)
-
-    def pair_copy(which, src, dst):
-        return pltpu.make_async_remote_copy(
-            src_ref=src, dst_ref=dst, send_sem=pair_send.at[which], recv_sem=pair_recv.at[which],
-            device_id=(me, tp, 1 - rep), device_id_type=MESH,
-        )
-
-    def seq_copy(phase, src, dst, hop):
-        target = seq_ahead(hop)
-        return pltpu.make_async_remote_copy(
-            src_ref=src(target), dst_ref=dst.at[me],
-            send_sem=seq_send.at[phase, hop], recv_sem=seq_recv.at[phase, hop],
-            device_id=(target, tp, rep), device_id_type=MESH,
-        )
-
-    def seq_start(phase, src, dst):
-        for hop in SEQ_HOPS:
-            seq_copy(phase, src, dst, hop).start()
-
-    def seq_wait(phase, src, dst):
-        for hop in SEQ_HOPS:
-            source = seq_behind(hop)
-            pltpu.make_async_remote_copy(
-                src_ref=src(source), dst_ref=dst.at[source],
-                send_sem=seq_send.at[phase, hop], recv_sem=seq_recv.at[phase, hop],
-                device_id=(source, tp, rep), device_id_type=MESH,
-            ).wait_recv()
-
-    def seq_sent(phase, src, dst):
-        for hop in SEQ_HOPS:
-            seq_copy(phase, src, dst, hop).wait_send()
-
-    src_state = lambda t: send_state.at[t]
-    src_slots = lambda t: send_slots.at[t]
-    src_soft = lambda t: send_soft.at[t]
-    src_back = lambda t: send_back.at[t]
-    src_result = lambda t: send_result
-    src_decode = lambda t: send_decode
-
-    def tp_copy(hop):
-        return pltpu.make_async_remote_copy(
-            src_ref=send_tp, dst_ref=sums_ref.at[tp],
-            send_sem=tp_send.at[hop], recv_sem=tp_recv.at[hop],
-            device_id=(me, lax.rem(tp + hop, TP), rep), device_id_type=MESH,
-        )
-
-    barrier = pltpu.get_barrier_semaphore()
-
-    for hop in SEQ_HOPS:
-        pl.semaphore_signal(
-            barrier, inc=1, device_id=(seq_ahead(hop), tp, rep), device_id_type=MESH
-        )
-    for hop in TP_HOPS:
-        pl.semaphore_signal(
-            barrier, inc=1, device_id=(me, lax.rem(tp + hop, TP), rep), device_id_type=MESH
-        )
-    pl.semaphore_signal(barrier, inc=1, device_id=(me, tp, 1 - rep), device_id_type=MESH)
 
     inputs["pages"].wait()
     ends = []

time: 35.6 us -> 35.9 us (level)
  no operation moved by 1% of the time
where the time goes in v6:
time: 35.9 us
  Pallas kernels  35.2 us (98%)
  between operations  0.64 us (2%)
    pallas_call x1, Pallas kernels, per_device(): pl.pallas_call(kernel, out_shape=(jax.ShapeDtypeStruct((ROWS, HEADS * DH)...  33.6 us
    pallas_call x1, Pallas kernels, per_device(): pl.pallas_call(norm_kernel, out_shape=(jax.ShapeDtypeStruct((ROWS, HEADS...  1.59 us

profile of v6, /device:TPU:1, one launch (start us, length us, event | category | flops | bytes accessed | tf_op | source)
XLA Modules:
  0.0 35.9 jit_solution(4962019442364497140)
XLA Ops:
  0.6 33.6 %attention_block.1 = (f32[1024,1024]{1,0:T(8,128)S(1)}, f32[8,16,128]{2,1,0:T(8,128)S(1)}, f32[16,64]{1,0:T(8,128)S(1)}, f32[16,8,128]{2,1,0:T(8,128)S(1)}, f32[8,128]{1,0:T(8,128)S(1)}) custom-call(s32[4]{0:T(128)} %pages_in.1, bf16[1024,1024]{1,0:T(8,128)(2,1)} %q_in.1, bf16[1024,1024]{1,0:T(8,128)(2,1)} %k_in.1, bf16[1024,1024]{1,0:T(8,128)(2,1)} %v_in.1, ...), custom_call_target="tpu_custom_call" | custom-call | tf_op jit(solution)/shard_map/attention_block/pallas_call | solution.py:628
  34.3 1.6 %norms.1 = (bf16[1024,1024]{1,0:T(8,128)(2,1)}, bf16[1,4,4,8,8]{4,3,2,1,0:T(8,128)(2,1)}, bf16[1,4,4,1024]{3,2,1,0:T(4,128)(2,1)}) custom-call(f32[1024,1024]{1,0:T(8,128)S(1)} %get-tuple-element.8.mixed, f32[8,16,128]{2,1,0:T(8,128)S(1)} %get-tuple-element.9.sums, f32[16,64]{1,0:T(8,128)S(1)} %get-tuple-element.10.decoded, f32[128,128]{1,0:T(8,128)S(1)} %bitcast.3, ...), custom_call_target="tpu_custom_call" | custom-call | tf_op jit(solution)/shard_map/norms/pallas_call | solution.py:716
